TPU v7x, 512 devices: a whole 4x4x16 slice. The times are simulated.
512 devices in a mesh: pm: 2 (over y_lo), ka: 128 (over x, z, core), isdf: 2 (over y_hi).
Axes of the slice: x: 4, y: 4 (y_hi: 2, y_lo: 2; y = y_hi * 2 + y_lo), z: 16, core: 2. Of those that a mesh axis runs over, the one named last changes fastest.
Arguments:
- amplitudes: bfloat16 [2, 2, 2, 256, 64, 256], P('pm', None, None, 'ka'), may hold values from -6 to 6
- conduction: bfloat16 [2, 256, 256, 512], P(None, 'ka', None, 'isdf'), may hold values from -0.375 to 0.375
- valence: bfloat16 [2, 256, 64, 512], P(None, 'ka'), may hold values from -0.75 to 0.75
- energy: float32 [256, 64, 256], P('ka', None, 'isdf'), may hold values from 0.5 to 2.5
- screened: bfloat16 [4, 2, 512, 512], P(None, None, 'isdf'), may hold values from -0.59765625 to 0.59765625
- coulomb: float32 [512, 512], P(None, 'isdf'), may hold values from -0.03125 to 0.03125
- mirror: int32 [256], P('ka'), may hold values from 0 to 255, as said below
- transfer_class: int32 [256, 256], P('ka'), may hold values from 0 to 3, as said below
Outputs:
- response: bfloat16 [2, 2, 2, 256, 64, 256], P('pm', None, None, 'ka', None, 'isdf')
Inputs may be any that keep to these rules, and one draw needn't show every extreme that they name: mirror[mirror[k]] = k; a k-point of block j (the aligned block of 2 k-points that holds it) has its mirror in block 127 - j. transfer_class[k, k2] depends only on (k - k2) mod 256.
All inputs are finite; a program needn't handle non-finite values.
Results may differ from a plain program's by a relative error of at most 0.015.
Values may be sent and summed in bfloat16 or wider, within the bound.
A program may use at most 128 MiB of HBM per device.

v0:
```python
import jax
import jax.numpy as jnp
from jax import lax
from jax.sharding import PartitionSpec as P

REACH = 2


HIGHEST = lax.Precision.HIGHEST


def swapped(block, axis, apart):
    count = lax.axis_size(axis)
    route = []
    for low in range(count):
        high = low | 1 << apart
        if high != low and high < count:
            route += [(low, high), (high, low)]
    return lax.ppermute(block, axis, route)


def shifted(value, axis, by):
    size = lax.axis_size(axis)
    return lax.ppermute(value, axis, [(i, (i + by) % size) for i in range(size)])


def pair_einsum(pattern, left, right, conjugate):

    def single(first, second):
        return jnp.einsum(pattern, first, second, preferred_element_type=jnp.float32)

    if conjugate:
        real_part = single(left[0], right[0]) + single(left[1], right[1])
        imag_part = single(left[1], right[0]) - single(left[0], right[1])
    else:
        real_part = single(left[0], right[0]) - single(left[1], right[1])
        imag_part = single(left[0], right[1]) + single(left[1], right[0])
    return (real_part, imag_part)


def conjugated(field):
    return jnp.stack([field[:, 0], -field[:, 1]], axis=1)


def coefficients(vector, conduction):
    real_part, imag_part = pair_einsum(
        "bkvc,kcm->bkvm", (vector[:, 0], vector[:, 1]), (conduction[0], conduction[1]), False
    )
    return jnp.stack([real_part, imag_part], axis=1).astype(jnp.bfloat16)


def amp_bits(field):
    for bit_number in range(lax.axis_size("ka").bit_length() - 1):
        field = swapped(field, "ka", bit_number)
    return field


def result_bits(field):
    for bit_number in range(lax.axis_size("ka").bit_length() - 1):
        field = swapped(field, "ka", bit_number)
    return field


def per_device(amplitudes, conduction, valence, energy, screened, coulomb, mirror, transfer_class):
    pm_index = lax.axis_index("pm")
    ka_index = lax.axis_index("ka")
    isdf_index = lax.axis_index("isdf")
    ka_count = lax.axis_size("ka")
    kpoint_count = conduction.shape[1]
    mu_count = conduction.shape[3]
    point_count = valence.shape[3]
    cond_share = energy.shape[2]
    vector_count = amplitudes.shape[1]
    is_plus = pm_index == 0
    parity = jnp.where(is_plus, 1.0, -1.0).astype(jnp.float32)
    exchange_weight = jnp.where(is_plus, 4.0, 0.0).astype(jnp.float32)
    local_amps = amplitudes[0]
    partner_amps = swapped(local_amps, "pm", 0)
    partner_side = jnp.where(is_plus, partner_amps, local_amps)
    distant_side = amp_bits(partner_side)
    direct = jnp.where(is_plus, local_amps, partner_amps).astype(jnp.float32)
    local_mirror = mirror - (ka_count - 1 - ka_index) * kpoint_count
    flipped = conjugated(jnp.take(distant_side, local_mirror, axis=2).astype(jnp.float32))
    vector = (direct + parity * flipped).astype(jnp.bfloat16)
    own_coef = coefficients(vector, conduction)
    valence_part = lax.dynamic_slice_in_dim(valence, isdf_index * mu_count, mu_count, 3)
    rho_real = jnp.einsum(
        "kvm,bkvm->bm", valence_part[0], own_coef[:, 0], preferred_element_type=jnp.float32
    )
    rho_real = rho_real + jnp.einsum(
        "kvm,bkvm->bm", valence_part[1], own_coef[:, 1], preferred_element_type=jnp.float32
    )
    rho_imag = jnp.einsum(
        "kvm,bkvm->bm", valence_part[0], own_coef[:, 1], preferred_element_type=jnp.float32
    )
    rho_imag = rho_imag - jnp.einsum(
        "kvm,bkvm->bm", valence_part[1], own_coef[:, 0], preferred_element_type=jnp.float32
    )
    density = jnp.stack([rho_real, rho_imag], axis=1)
    spread = jnp.einsum("nm,brm->brn", coulomb, density, precision=HIGHEST)
    spread = lax.psum(spread, ("ka", "isdf"))
    potential = lax.dynamic_slice_in_dim(spread, isdf_index * mu_count, mu_count, 2)
    class_ids = jnp.arange(screened.shape[0], dtype=jnp.int32)

    def accumulate(totals, coef_block, valence_block, source):
        pair_real, pair_imag = pair_einsum(
            "bqvm,qvn->bqmn",
            (coef_block[:, 0], coef_block[:, 1]),
            (valence_block[0], valence_block[1]),
            True,
        )
        pair_real = pair_real.astype(jnp.bfloat16)
        pair_imag = pair_imag.astype(jnp.bfloat16)
        classes = lax.dynamic_slice_in_dim(transfer_class, source * kpoint_count, kpoint_count, 1)
        selector = (classes[:, :, None] == class_ids).astype(jnp.bfloat16)
        total_real, total_imag = totals
        for visitor in range(kpoint_count):
            chosen = jnp.einsum(
                "kw,wrmn->rkmn", selector[:, visitor], screened, preferred_element_type=jnp.float32
            ).astype(jnp.bfloat16)
            screen_real = chosen[0][None].astype(jnp.float32)
            screen_imag = chosen[1][None].astype(jnp.float32)
            visit_real = pair_real[:, visitor][:, None].astype(jnp.float32)
            visit_imag = pair_imag[:, visitor][:, None].astype(jnp.float32)
            total_real = total_real + (screen_real * visit_real - screen_imag * visit_imag)
            total_imag = total_imag + (screen_real * visit_imag + screen_imag * visit_real)
        return (total_real, total_imag)

    payload = (vector, conduction, valence)

    def advance(moving, offset):
        return shifted((moving[0], moving[1], moving[2]), "ka", offset)

    def unpack(moving):
        return (coefficients(moving[0], moving[1]), moving[2])

    def visit(totals, moving, distance):
        coef_block, valence_block = unpack(moving)
        source = jnp.mod(ka_index + distance, ka_count)
        return accumulate(totals, coef_block, valence_block, source)

    zero_field = jnp.zeros((vector_count, kpoint_count, mu_count, point_count), jnp.float32)
    totals = accumulate((zero_field, zero_field), own_coef, valence, ka_index)
    below_item = payload
    for count_done in range(REACH):
        below_item = advance(below_item, 1)
        totals = visit(totals, below_item, -(count_done + 1))
    above_item = payload
    for count_done in range(REACH):
        above_item = advance(above_item, -1)
        totals = visit(totals, above_item, count_done + 1)
    sum_real = totals[0].astype(jnp.bfloat16)
    sum_imag = totals[1].astype(jnp.bfloat16)
    back_real, back_imag = pair_einsum(
        "bkmn,kvn->bkvm", (sum_real, sum_imag), (valence[0], valence[1]), False
    )
    potential_real = potential[:, 0][:, None, None, :]
    potential_imag = potential[:, 1][:, None, None, :]
    exchange_real = potential_real * valence_part[0] - potential_imag * valence_part[1]
    exchange_imag = potential_real * valence_part[1] + potential_imag * valence_part[0]
    field_real = (exchange_weight * exchange_real - back_real).astype(jnp.bfloat16)
    field_imag = (exchange_weight * exchange_imag - back_imag).astype(jnp.bfloat16)
    out_real, out_imag = pair_einsum(
        "bkvm,kcm->bkvc", (field_real, field_imag), (conduction[0], conduction[1]), True
    )
    partial_out = jnp.stack([out_real, out_imag], axis=1)
    summed = lax.psum_scatter(
        partial_out.astype(jnp.bfloat16), "isdf", scatter_dimension=4, tiled=True
    ).astype(jnp.float32)
    vector_part = lax.dynamic_slice_in_dim(vector, isdf_index * cond_share, cond_share, 4).astype(
        jnp.float32
    )
    channel_out = (energy[None, None] * vector_part + summed).astype(jnp.bfloat16)
    partner_out = swapped(channel_out, "pm", 0)
    blended = (
        0.5 * (partner_out.astype(jnp.float32) + parity * channel_out.astype(jnp.float32))
    ).astype(jnp.bfloat16)
    distant_out = result_bits(blended)
    reflected = conjugated(jnp.take(distant_out, local_mirror, axis=2))
    result = jnp.where(is_plus, blended, reflected)
    return result[None]


def solution(mesh):
    return jax.shard_map(
        per_device,
        mesh=mesh,
        in_specs=(
            P("pm", None, None, "ka", None, None),
            P(None, "ka", None, "isdf"),
            P(None, "ka", None, None),
            P("ka", None, "isdf"),
            P(None, None, "isdf", None),
            P(None, "isdf"),
            P("ka"),
            P("ka", None),
        ),
        out_specs=P("pm", None, None, "ka", None, "isdf"),
        check_vma=False,
    )
```

profile of v0, /device:TPU:25, one launch (start us, length us, event | category | flops | bytes accessed | tf_op | source)
XLA Modules:
  0.0 1085.5 jit_solution(7875653439164302398)
XLA Ops:
  6.5 4.2 collective-permute-start.9
  12.7 3.6 collective-permute-start.10
  16.4 9.8 collective-permute-start.16
  30.7 3.2 copy.91
  57.0 3.0 fusion.79
  66.3 7.3 collective-permute-start.1
  79.9 5.8 collective-permute-done.2
  89.6 12.6 %collective-permute-done.3 = bf16[2,2,2,64,256]{4,3,0,2,1:T(8,128)(2,1)S(1)} collective-permute-done((bf16[2,2,2,64,256]{4,3,0,2,1:T(8,128)(2,1)S(1)}, bf16[2,2,2,64,256]{4,3,0,2,1:T(8,128)(2,1)S(1)}, u32[]{:S(2)}, u32[]{:S(2)}) %collective-permute-start.3) | collective-permute-done | bytes 262176 | tf_op jit(solution)/shard_map/ppermute | solution.py:19
  106.2 28.8 %collective-permute-done.4 = bf16[2,2,2,64,256]{4,3,0,2,1:T(8,128)(2,1)S(1)} collective-permute-done((bf16[2,2,2,64,256]{4,3,0,2,1:T(8,128)(2,1)S(1)}, bf16[2,2,2,64,256]{4,3,0,2,1:T(8,128)(2,1)S(1)}, u32[]{:S(2)}, u32[]{:S(2)}) %collective-permute-start.4) | collective-permute-done | bytes 262176 | tf_op jit(solution)/shard_map/ppermute | solution.py:19
  139.0 18.7 %collective-permute-done.5 = bf16[2,2,2,64,256]{4,3,0,2,1:T(8,128)(2,1)S(1)} collective-permute-done((bf16[2,2,2,64,256]{4,3,0,2,1:T(8,128)(2,1)S(1)}, bf16[2,2,2,64,256]{4,3,0,2,1:T(8,128)(2,1)S(1)}, u32[]{:S(2)}, u32[]{:S(2)}) %collective-permute-start.5) | collective-permute-done | bytes 262176 | tf_op jit(solution)/shard_map/ppermute | solution.py:19
  162.9 4.1 collective-permute-done.6
  167.0 5.0 collective-permute-start.7
  198.2 3.6 collective-permute-start.19
  203.8 6.9 collective-permute-start.18
  226.9 656.3 %psum.7 = f32[2,2,512]{2,1,0:T(2,128)S(1)} all-reduce(f32[2,2,512]{2,1,0:T(2,128)S(1)} %fusion.90), channel_id=1, replica_groups=mesh['pm'=2,'ka'=128,'isdf'=2] {'ka','isdf'}, use_global_device_ids=true, to_apply=%region_0.1 | all-reduce | flops 2048 | bytes 16384 | tf_op jit(solution)/shard_map/psum | solution.py:101
  887.7 6.5 collective-permute-start.14
  921.3 4.9 collective-permute-start.17
  953.9 9.2 add_convert_fusion
  963.2 9.5 add_convert_fusion.1
  977.1 15.5 %reduce-scatter.4.cloned.1.call-done = bf16[128,512]{1,0:T(8,128)(2,1)} async-done(((bf16[256,512]{1,0:T(8,128)(2,1)}), bf16[128,512]{1,0:T(8,128)(2,1)}) %reduce-scatter.4.cloned.1.call-update) | async-done | bytes 131088
  996.8 4.3 collective-permute-done.20
  1001.2 3.4 collective-permute-start.21
  1005.6 3.2 collective-permute-start.22
  1008.8 3.4 collective-permute-done.22
  1012.2 4.2 collective-permute-start.23
  1016.4 5.8 collective-permute-done.23
  1022.2 7.3 collective-permute-start.24
  1029.5 10.5 collective-permute-done.24
  1040.0 12.5 %collective-permute-start.25 = (bf16[2,2,2,64,128]{4,3,0,2,1:T(8,128)(2,1)S(1)}, bf16[2,2,2,64,128]{4,3,0,2,1:T(8,128)(2,1)S(1)}, u32[]{:S(2)}, u32[]{:S(2)}) collective-permute-start(bf16[2,2,2,64,128]{4,3,0,2,1:T(8,128)(2,1)S(1)} %collective-permute-done.24), channel_id=1, source_target_pairs={{0,32},{32,0},{2,34},{34,2},{4,36},{36,4},{6,38},{38,6},{8,40},{40... | collective-permute-start | bytes 393224 | tf_op jit(solution)/shard_map/ppermute | solution.py:19
  1052.5 11.7 %collective-permute-done.25 = bf16[2,2,2,64,128]{4,3,0,2,1:T(8,128)(2,1)S(1)} collective-permute-done((bf16[2,2,2,64,128]{4,3,0,2,1:T(8,128)(2,1)S(1)}, bf16[2,2,2,64,128]{4,3,0,2,1:T(8,128)(2,1)S(1)}, u32[]{:S(2)}, u32[]{:S(2)}) %collective-permute-start.25) | collective-permute-done | bytes 131104 | tf_op jit(solution)/shard_map/ppermute | solution.py:19
  1064.1 3.0 collective-permute-start.26
  1069.8 4.4 collective-permute-start.27
  (285 shorter events, 178.3 us)
Async XLA Ops:
  6.5 219.8 %copy-start = (f32[512,256]{1,0:T(8,128)S(1)}, f32[512,256]{1,0:T(8,128)}, u32[]{:S(2)}) copy-start(f32[512,256]{1,0:T(8,128)} %param.13) | copy-start | bytes 1572868
  6.5 986.1 %reduce-scatter.4.cloned.1.call-start = ((), (), s32[]{:S(2)}) async-start(), calls=%async_computation.1 | async-start | bytes 393216
  6.5 195.2 %collective-permute-start.9 = (bf16[2,2,256,256]{3,2,1,0:T(8,128)(2,1)}, bf16[2,2,256,256]{3,2,1,0:T(8,128)(2,1)}, u32[]{:S(2)}, u32[]{:S(2)}) collective-permute-start(bf16[2,2,256,256]{3,2,1,0:T(8,128)(2,1)} %param.9), channel_id=1, source_target_pairs={{0,2},{2,4},{4,6},{6,8},{8,10},{10,12},{12,14},{14,16},{16,18},{18... | collective-permute-start | bytes 1572872 | tf_op jit(solution)/shard_map/ppermute | solution.py:24
  10.8 193.0 %collective-permute-start.15 = (bf16[2,2,256,256]{3,2,1,0:T(8,128)(2,1)}, bf16[2,2,256,256]{3,2,1,0:T(8,128)(2,1)}, u32[]{:S(2)}, u32[]{:S(2)}) collective-permute-start(bf16[2,2,256,256]{3,2,1,0:T(8,128)(2,1)} %param.9), channel_id=1, source_target_pairs={{0,254},{2,0},{4,2},{6,4},{8,6},{10,8},{12,10},{14,12},{16,14},{18... | collective-permute-start | bytes 1572872 | tf_op jit(solution)/shard_map/ppermute | solution.py:24
  12.7 183.4 %collective-permute-start.10 = (bf16[2,2,64,512]{3,2,1,0:T(8,128)(2,1)}, bf16[2,2,64,512]{3,2,1,0:T(8,128)(2,1)}, u32[]{:S(2)}, u32[]{:S(2)}) collective-permute-start(bf16[2,2,64,512]{3,2,1,0:T(8,128)(2,1)} %param.10), channel_id=1, source_target_pairs={{0,2},{2,4},{4,6},{6,8},{8,10},{10,12},{12,14},{14,16},{16,18},{18... | collective-permute-start | bytes 786440 | tf_op jit(solution)/shard_map/ppermute | solution.py:24
  16.4 181.8 %collective-permute-start.16 = (bf16[2,2,64,512]{3,2,1,0:T(8,128)(2,1)}, bf16[2,2,64,512]{3,2,1,0:T(8,128)(2,1)}, u32[]{:S(2)}, u32[]{:S(2)}) collective-permute-start(bf16[2,2,64,512]{3,2,1,0:T(8,128)(2,1)} %param.10), channel_id=1, source_target_pairs={{0,254},{2,0},{4,2},{6,4},{8,6},{10,8},{12,10},{14,12},{16,14},{18... | collective-permute-start | bytes 786440 | tf_op jit(solution)/shard_map/ppermute | solution.py:24
  27.1 39.1 %collective-permute-start = (bf16[2,2,2,64,256]{4,3,0,2,1:T(8,128)(2,1)S(1)}, bf16[2,2,2,64,256]{4,3,0,2,1:T(8,128)(2,1)S(1)}, u32[]{:S(2)}, u32[]{:S(2)}) collective-permute-start(bf16[2,2,2,64,256]{4,3,0,2,1:T(8,128)(2,1)S(1)} %bitcast.651), channel_id=1, source_target_pairs={{0,256},{256,0},{1,257},{257,1},{2,258},{258,2},{3,259},{259,3},{4... | collective-permute-start | bytes 786440 | tf_op jit(solution)/shard_map/ppermute | solution.py:19
  66.3 9.5 collective-permute-start.1
  75.7 9.9 collective-permute-start.2
  85.7 16.6 %collective-permute-start.3 = (bf16[2,2,2,64,256]{4,3,0,2,1:T(8,128)(2,1)S(1)}, bf16[2,2,2,64,256]{4,3,0,2,1:T(8,128)(2,1)S(1)}, u32[]{:S(2)}, u32[]{:S(2)}) collective-permute-start(bf16[2,2,2,64,256]{4,3,0,2,1:T(8,128)(2,1)S(1)} %collective-permute-done.2), channel_id=1, source_target_pairs={{0,8},{8,0},{2,10},{10,2},{4,12},{12,4},{6,14},{14,6},{16,24},{24,... | collective-permute-start | bytes 786440 | tf_op jit(solution)/shard_map/ppermute | solution.py:19
  102.2 32.8 %collective-permute-start.4 = (bf16[2,2,2,64,256]{4,3,0,2,1:T(8,128)(2,1)S(1)}, bf16[2,2,2,64,256]{4,3,0,2,1:T(8,128)(2,1)S(1)}, u32[]{:S(2)}, u32[]{:S(2)}) collective-permute-start(bf16[2,2,2,64,256]{4,3,0,2,1:T(8,128)(2,1)S(1)} %collective-permute-done.3), channel_id=1, source_target_pairs={{0,16},{16,0},{2,18},{18,2},{4,20},{20,4},{6,22},{22,6},{8,24},{24... | collective-permute-start | bytes 786440 | tf_op jit(solution)/shard_map/ppermute | solution.py:19
  135.0 22.7 %collective-permute-start.5 = (bf16[2,2,2,64,256]{4,3,0,2,1:T(8,128)(2,1)S(1)}, bf16[2,2,2,64,256]{4,3,0,2,1:T(8,128)(2,1)S(1)}, u32[]{:S(2)}, u32[]{:S(2)}) collective-permute-start(bf16[2,2,2,64,256]{4,3,0,2,1:T(8,128)(2,1)S(1)} %collective-permute-done.4), channel_id=1, source_target_pairs={{0,32},{32,0},{2,34},{34,2},{4,36},{36,4},{6,38},{38,6},{8,40},{40... | collective-permute-start | bytes 786440 | tf_op jit(solution)/shard_map/ppermute | solution.py:19
  157.8 9.2 collective-permute-start.6
  167.0 43.7 %collective-permute-start.7 = (bf16[2,2,2,64,256]{4,3,0,2,1:T(8,128)(2,1)}, bf16[2,2,2,64,256]{4,3,0,2,1:T(8,128)(2,1)}, u32[]{:S(2)}, u32[]{:S(2)}) collective-permute-start(bf16[2,2,2,64,256]{4,3,0,2,1:T(8,128)(2,1)} %collective-permute-done.6), channel_id=1, source_target_pairs={{0,128},{128,0},{2,130},{130,2},{4,132},{132,4},{6,134},{134,6},{8... | collective-permute-start | bytes 786440 | tf_op jit(solution)/shard_map/ppermute | solution.py:19
  196.1 734.7 %collective-permute-start.13 = (bf16[2,2,64,512]{3,2,1,0:T(8,128)(2,1)}, bf16[2,2,64,512]{3,2,1,0:T(8,128)(2,1)}, u32[]{:S(2)}, u32[]{:S(2)}) collective-permute-start(bf16[2,2,64,512]{3,2,1,0:T(8,128)(2,1)} %collective-permute-done.10), channel_id=1, source_target_pairs={{0,2},{2,4},{4,6},{6,8},{8,10},{10,12},{12,14},{14,16},{16,18},{18... | collective-permute-start | bytes 786440 | tf_op jit(solution)/shard_map/ppermute | solution.py:24
  198.2 745.1 %collective-permute-start.19 = (bf16[2,2,64,512]{3,2,1,0:T(8,128)(2,1)}, bf16[2,2,64,512]{3,2,1,0:T(8,128)(2,1)}, u32[]{:S(2)}, u32[]{:S(2)}) collective-permute-start(bf16[2,2,64,512]{3,2,1,0:T(8,128)(2,1)} %collective-permute-done.16), channel_id=1, source_target_pairs={{0,254},{2,0},{4,2},{6,4},{8,6},{10,8},{12,10},{14,12},{16,14},{18... | collective-permute-start | bytes 786440 | tf_op jit(solution)/shard_map/ppermute | solution.py:24
  201.7 719.6 %collective-permute-start.12 = (bf16[2,2,256,256]{3,2,1,0:T(8,128)(2,1)}, bf16[2,2,256,256]{3,2,1,0:T(8,128)(2,1)}, u32[]{:S(2)}, u32[]{:S(2)}) collective-permute-start(bf16[2,2,256,256]{3,2,1,0:T(8,128)(2,1)} %collective-permute-done.9), channel_id=1, source_target_pairs={{0,2},{2,4},{4,6},{6,8},{8,10},{10,12},{12,14},{14,16},{16,18},{18... | collective-permute-start | bytes 1572872 | tf_op jit(solution)/shard_map/ppermute | solution.py:24
  203.8 734.8 %collective-permute-start.18 = (bf16[2,2,256,256]{3,2,1,0:T(8,128)(2,1)}, bf16[2,2,256,256]{3,2,1,0:T(8,128)(2,1)}, u32[]{:S(2)}, u32[]{:S(2)}) collective-permute-start(bf16[2,2,256,256]{3,2,1,0:T(8,128)(2,1)} %collective-permute-done.15), channel_id=1, source_target_pairs={{0,254},{2,0},{4,2},{6,4},{8,6},{10,8},{12,10},{14,12},{16,14},{18... | collective-permute-start | bytes 1572872 | tf_op jit(solution)/shard_map/ppermute | solution.py:24
  219.7 667.9 %collective-permute-start.8 = (bf16[2,2,2,64,256]{4,3,0,2,1:T(8,128)(2,1)}, bf16[2,2,2,64,256]{4,3,0,2,1:T(8,128)(2,1)}, u32[]{:S(2)}, u32[]{:S(2)}) collective-permute-start(bf16[2,2,2,64,256]{4,3,0,2,1:T(8,128)(2,1)} %fusion.89), channel_id=1, source_target_pairs={{0,2},{2,4},{4,6},{6,8},{8,10},{10,12},{12,14},{14,16},{16,18},{18... | collective-permute-start | bytes 786440 | tf_op jit(solution)/shard_map/ppermute | solution.py:24
  226.9 657.9 %copy-start.45 = (bf16[2,2,64,256]{3,2,1,0:T(8,128)(2,1)S(1)}, bf16[2,2,64,256]{3,2,1,0:T(8,128)(2,1)}, u32[]{:S(2)}) copy-start(bf16[2,2,64,256]{3,2,1,0:T(8,128)(2,1)} %get-tuple-element.66) | copy-start | bytes 393220
  887.7 19.2 %collective-permute-start.14 = (bf16[2,2,2,64,256]{4,3,0,2,1:T(8,128)(2,1)}, bf16[2,2,2,64,256]{4,3,0,2,1:T(8,128)(2,1)S(1)}, u32[]{:S(2)}, u32[]{:S(2)}) collective-permute-start(bf16[2,2,2,64,256]{4,3,0,2,1:T(8,128)(2,1)} %fusion.89), channel_id=1, source_target_pairs={{0,254},{2,0},{4,2},{6,4},{8,6},{10,8},{12,10},{14,12},{16,14},{18... | collective-permute-start | bytes 786440 | tf_op jit(solution)/shard_map/ppermute | solution.py:24
  906.9 19.4 %collective-permute-start.11 = (bf16[2,2,2,64,256]{4,3,0,2,1:T(8,128)(2,1)}, bf16[2,2,2,64,256]{4,3,0,2,1:T(8,128)(2,1)S(1)}, u32[]{:S(2)}, u32[]{:S(2)}) collective-permute-start(bf16[2,2,2,64,256]{4,3,0,2,1:T(8,128)(2,1)} %collective-permute-done.8), channel_id=1, source_target_pairs={{0,2},{2,4},{4,6},{6,8},{8,10},{10,12},{12,14},{14,16},{16,18},{18... | collective-permute-start | bytes 786440 | tf_op jit(solution)/shard_map/ppermute | solution.py:24
  921.3 17.3 %collective-permute-start.17 = (bf16[2,2,2,64,256]{4,3,0,2,1:T(8,128)(2,1)S(1)}, bf16[2,2,2,64,256]{4,3,0,2,1:T(8,128)(2,1)S(1)}, u32[]{:S(2)}, u32[]{:S(2)}) collective-permute-start(bf16[2,2,2,64,256]{4,3,0,2,1:T(8,128)(2,1)S(1)} %collective-permute-done.14), channel_id=1, source_target_pairs={{0,254},{2,0},{4,2},{6,4},{8,6},{10,8},{12,10},{14,12},{16,14},{18... | collective-permute-start | bytes 786440 | tf_op jit(solution)/shard_map/ppermute | solution.py:24
  976.0 102.4 %copy-start.1 = (f32[512,256]{1,0:T(8,128)S(1)}, f32[512,256]{1,0:T(8,128)}, u32[]{:S(2)}) copy-start(f32[512,256]{1,0:T(8,128)} %param.13) | copy-start | bytes 1572868
  994.8 6.3 collective-permute-start.20
  1001.2 4.4 collective-permute-start.21
  1005.6 6.6 collective-permute-start.22
  1012.2 10.0 collective-permute-start.23
  1022.2 17.8 %collective-permute-start.24 = (bf16[2,2,2,64,128]{4,3,0,2,1:T(8,128)(2,1)S(1)}, bf16[2,2,2,64,128]{4,3,0,2,1:T(8,128)(2,1)S(1)}, u32[]{:S(2)}, u32[]{:S(2)}) collective-permute-start(bf16[2,2,2,64,128]{4,3,0,2,1:T(8,128)(2,1)S(1)} %collective-permute-done.23), channel_id=1, source_target_pairs={{0,16},{16,0},{2,18},{18,2},{4,20},{20,4},{6,22},{22,6},{8,24},{24... | collective-permute-start | bytes 393224 | tf_op jit(solution)/shard_map/ppermute | solution.py:19
  1040.0 24.2 %collective-permute-start.25 = (bf16[2,2,2,64,128]{4,3,0,2,1:T(8,128)(2,1)S(1)}, bf16[2,2,2,64,128]{4,3,0,2,1:T(8,128)(2,1)S(1)}, u32[]{:S(2)}, u32[]{:S(2)}) collective-permute-start(bf16[2,2,2,64,128]{4,3,0,2,1:T(8,128)(2,1)S(1)} %collective-permute-done.24), channel_id=1, source_target_pairs={{0,32},{32,0},{2,34},{34,2},{4,36},{36,4},{6,38},{38,6},{8,40},{40... | collective-permute-start | bytes 393224 | tf_op jit(solution)/shard_map/ppermute | solution.py:19
  1064.1 5.7 collective-permute-start.26
  1069.8 7.2 collective-permute-start.27
  (57 other events, 482.1 us)
Sparse Core Ops, SparseCore 0:
  977.2 15.3 reduce-scatter.3
where the time goes:
time: 1100 us; the launch traced here: 1090 us
  blocking collectives  656 us (60%)
  waiting for transfers between devices  128 us (12%)
  starting transfers between devices  115 us (10%)
  matrix products  76.3 us (7%)
  other arithmetic  56.6 us (5%)
  local copies, waits for them, and re-layouts  38.9 us (4%)
  between operations  14.8 us (1%)
    psum x1, blocking collectives, per_device(): spread = lax.psum(spread, ('ka', 'isdf'))  656 us
    ppermute x16, waiting for transfers between devices, swapped(): return lax.ppermute(block, axis, route)  112 us
    ppermute x16, starting transfers between devices, swapped(): return lax.ppermute(block, axis, route)  65.3 us
    dot_general x48, matrix products, single(): jnp.einsum(pattern, first, second, preferred_element_type=jnp.float32)  53.3 us
    ppermute x12, starting transfers between devices, shifted(): lax.ppermute(value, axis, [(i, (i + by) % size) for i in range(size)])  49.5 us
    dot_general x10, matrix products, accumulate(): jnp.einsum('kw,wrmn->rkmn', selector[:, visitor], screened, preferred_ele...  22.4 us
  transfers between devices with their start and end apart: 29, of which 14 were waited for; matrix products, arithmetic and copies ran while one was open for 12% of the time, Pallas kernels for 0%

commit v1 on v0

--- a/solution.py
+++ b/solution.py
@@ -59,6 +59,11 @@
     for bit_number in range(lax.axis_size("ka").bit_length() - 1):
         field = swapped(field, "ka", bit_number)
     return field
+
+
+def by_mirror(field, local_mirror):
+    index = local_mirror[None, None, :, None, None]
+    return jnp.where(index == 0, field[:, :, 0:1], field[:, :, 1:2])
 
 
 def per_device(amplitudes, conduction, valence, energy, screened, coulomb, mirror, transfer_class):
@@ -80,7 +85,7 @@
     distant_side = amp_bits(partner_side)
     direct = jnp.where(is_plus, local_amps, partner_amps).astype(jnp.float32)
     local_mirror = mirror - (ka_count - 1 - ka_index) * kpoint_count
-    flipped = conjugated(jnp.take(distant_side, local_mirror, axis=2).astype(jnp.float32))
+    flipped = conjugated(by_mirror(distant_side, local_mirror).astype(jnp.float32))
     vector = (direct + parity * flipped).astype(jnp.bfloat16)
     own_coef = coefficients(vector, conduction)
     valence_part = lax.dynamic_slice_in_dim(valence, isdf_index * mu_count, mu_count, 3)
@@ -176,7 +181,7 @@
         0.5 * (partner_out.astype(jnp.float32) + parity * channel_out.astype(jnp.float32))
     ).astype(jnp.bfloat16)
     distant_out = result_bits(blended)
-    reflected = conjugated(jnp.take(distant_out, local_mirror, axis=2))
+    reflected = conjugated(by_mirror(distant_out, local_mirror))
     result = jnp.where(is_plus, blended, reflected)
     return result[None]
 

time: 1100 us -> 1100 us (level)
  no operation moved by 1% of the time
where the time goes in v1:
time: 1100 us; the launch traced here: 1080 us
  blocking collectives  656 us (60%)
  waiting for transfers between devices  128 us (12%)
  starting transfers between devices  115 us (10%)
  matrix products  76.3 us (7%)
  other arithmetic  56 us (5%)
  local copies, waits for them, and re-layouts  35.4 us (3%)
  between operations  15.1 us (1%)
    psum x1, blocking collectives, per_device(): spread = lax.psum(spread, ('ka', 'isdf'))  656 us
    ppermute x16, waiting for transfers between devices, swapped(): return lax.ppermute(block, axis, route)  112 us
    ppermute x16, starting transfers between devices, swapped(): return lax.ppermute(block, axis, route)  65.4 us
    dot_general x48, matrix products, single(): jnp.einsum(pattern, first, second, preferred_element_type=jnp.float32)  53.4 us
    ppermute x12, starting transfers between devices, shifted(): lax.ppermute(value, axis, [(i, (i + by) % size) for i in range(size)])  49.6 us
    mul x10, other arithmetic, accumulate(): screen_real * visit_real - screen_imag * visit_imag  23 us
    dot_general x10, matrix products, accumulate(): jnp.einsum('kw,wrmn->rkmn', selector[:, visitor], screened, preferred_ele...  22.4 us
  transfers between devices with their start and end apart: 29, of which 14 were waited for; matrix products, arithmetic and copies ran while one was open for 12% of the time, Pallas kernels for 0%

profile of v1, /device:TPU:25, one launch (start us, length us, event | category | flops | bytes accessed | tf_op | source)
XLA Modules:
  0.0 1081.5 jit_solution(11353441118219177994)
XLA Ops:
  6.5 4.2 collective-permute-start.9
  12.7 3.6 collective-permute-start.10
  16.4 9.8 collective-permute-start.16
  30.7 3.2 copy.48
  64.1 3.5 fusion.75
  67.7 7.3 collective-permute-start.1
  81.2 5.8 collective-permute-done.2
  91.0 12.6 %collective-permute-done.3 = bf16[2,2,2,64,256]{4,3,0,2,1:T(8,128)(2,1)S(1)} collective-permute-done((bf16[2,2,2,64,256]{4,3,0,2,1:T(8,128)(2,1)S(1)}, bf16[2,2,2,64,256]{4,3,0,2,1:T(8,128)(2,1)S(1)}, u32[]{:S(2)}, u32[]{:S(2)}) %collective-permute-start.3) | collective-permute-done | bytes 262176 | tf_op jit(solution)/shard_map/ppermute | solution.py:19
  107.5 28.8 %collective-permute-done.4 = bf16[2,2,2,64,256]{4,3,0,2,1:T(8,128)(2,1)S(1)} collective-permute-done((bf16[2,2,2,64,256]{4,3,0,2,1:T(8,128)(2,1)S(1)}, bf16[2,2,2,64,256]{4,3,0,2,1:T(8,128)(2,1)S(1)}, u32[]{:S(2)}, u32[]{:S(2)}) %collective-permute-start.4) | collective-permute-done | bytes 262176 | tf_op jit(solution)/shard_map/ppermute | solution.py:19
  140.3 18.8 %collective-permute-done.5 = bf16[2,2,2,64,256]{4,3,0,2,1:T(8,128)(2,1)S(1)} collective-permute-done((bf16[2,2,2,64,256]{4,3,0,2,1:T(8,128)(2,1)S(1)}, bf16[2,2,2,64,256]{4,3,0,2,1:T(8,128)(2,1)S(1)}, u32[]{:S(2)}, u32[]{:S(2)}) %collective-permute-start.5) | collective-permute-done | bytes 262176 | tf_op jit(solution)/shard_map/ppermute | solution.py:19
  164.1 4.2 collective-permute-done.6
  168.3 4.8 collective-permute-start.7
  199.2 3.6 collective-permute-start.19
  204.8 6.9 collective-permute-start.18
  223.1 656.3 %psum.7 = f32[2,2,512]{2,1,0:T(2,128)S(1)} all-reduce(f32[2,2,512]{2,1,0:T(2,128)S(1)} %fusion.90), channel_id=1, replica_groups=mesh['pm'=2,'ka'=128,'isdf'=2] {'ka','isdf'}, use_global_device_ids=true, to_apply=%region_0.1 | all-reduce | flops 2048 | bytes 16384 | tf_op jit(solution)/shard_map/psum | solution.py:106
  883.9 6.5 collective-permute-start.14
  917.7 4.9 collective-permute-start.17
  950.3 9.2 add_convert_fusion
  959.6 9.5 add_convert_fusion.1
  973.5 15.5 %reduce-scatter.4.cloned.1.call-done = bf16[128,512]{1,0:T(8,128)(2,1)} async-done(((bf16[256,512]{1,0:T(8,128)(2,1)}), bf16[128,512]{1,0:T(8,128)(2,1)}) %reduce-scatter.4.cloned.1.call-update) | async-done | bytes 131088
  993.2 4.3 collective-permute-done.20
  997.6 3.4 collective-permute-start.21
  1002.0 3.2 collective-permute-start.22
  1005.2 3.4 collective-permute-done.22
  1008.6 4.2 collective-permute-start.23
  1012.8 5.8 collective-permute-done.23
  1018.6 7.3 collective-permute-start.24
  1025.9 10.5 collective-permute-done.24
  1036.4 12.5 %collective-permute-start.25 = (bf16[2,2,2,64,128]{4,3,0,2,1:T(8,128)(2,1)S(1)}, bf16[2,2,2,64,128]{4,3,0,2,1:T(8,128)(2,1)S(1)}, u32[]{:S(2)}, u32[]{:S(2)}) collective-permute-start(bf16[2,2,2,64,128]{4,3,0,2,1:T(8,128)(2,1)S(1)} %collective-permute-done.24), channel_id=1, source_target_pairs={{0,32},{32,0},{2,34},{34,2},{4,36},{36,4},{6,38},{38,6},{8,40},{40... | collective-permute-start | bytes 393224 | tf_op jit(solution)/shard_map/ppermute | solution.py:19
  1048.9 11.7 %collective-permute-done.25 = bf16[2,2,2,64,128]{4,3,0,2,1:T(8,128)(2,1)S(1)} collective-permute-done((bf16[2,2,2,64,128]{4,3,0,2,1:T(8,128)(2,1)S(1)}, bf16[2,2,2,64,128]{4,3,0,2,1:T(8,128)(2,1)S(1)}, u32[]{:S(2)}, u32[]{:S(2)}) %collective-permute-start.25) | collective-permute-done | bytes 131104 | tf_op jit(solution)/shard_map/ppermute | solution.py:19
  1060.5 3.1 collective-permute-start.26
  1066.2 4.6 collective-permute-start.27
  (284 shorter events, 173.5 us)
Async XLA Ops:
  6.5 216.1 %copy-start = (f32[512,256]{1,0:T(8,128)S(1)}, f32[512,256]{1,0:T(8,128)}, u32[]{:S(2)}) copy-start(f32[512,256]{1,0:T(8,128)} %param.13) | copy-start | bytes 1572868
  6.5 982.5 %reduce-scatter.4.cloned.1.call-start = ((), (), s32[]{:S(2)}) async-start(), calls=%async_computation.1 | async-start | bytes 393216
  6.5 196.3 %collective-permute-start.9 = (bf16[2,2,256,256]{3,2,1,0:T(8,128)(2,1)}, bf16[2,2,256,256]{3,2,1,0:T(8,128)(2,1)}, u32[]{:S(2)}, u32[]{:S(2)}) collective-permute-start(bf16[2,2,256,256]{3,2,1,0:T(8,128)(2,1)} %param.9), channel_id=1, source_target_pairs={{0,2},{2,4},{4,6},{6,8},{8,10},{10,12},{12,14},{14,16},{16,18},{18... | collective-permute-start | bytes 1572872 | tf_op jit(solution)/shard_map/ppermute | solution.py:24
  10.8 194.0 %collective-permute-start.15 = (bf16[2,2,256,256]{3,2,1,0:T(8,128)(2,1)}, bf16[2,2,256,256]{3,2,1,0:T(8,128)(2,1)}, u32[]{:S(2)}, u32[]{:S(2)}) collective-permute-start(bf16[2,2,256,256]{3,2,1,0:T(8,128)(2,1)} %param.9), channel_id=1, source_target_pairs={{0,254},{2,0},{4,2},{6,4},{8,6},{10,8},{12,10},{14,12},{16,14},{18... | collective-permute-start | bytes 1572872 | tf_op jit(solution)/shard_map/ppermute | solution.py:24
  12.7 184.4 %collective-permute-start.10 = (bf16[2,2,64,512]{3,2,1,0:T(8,128)(2,1)}, bf16[2,2,64,512]{3,2,1,0:T(8,128)(2,1)}, u32[]{:S(2)}, u32[]{:S(2)}) collective-permute-start(bf16[2,2,64,512]{3,2,1,0:T(8,128)(2,1)} %param.10), channel_id=1, source_target_pairs={{0,2},{2,4},{4,6},{6,8},{8,10},{10,12},{12,14},{14,16},{16,18},{18... | collective-permute-start | bytes 786440 | tf_op jit(solution)/shard_map/ppermute | solution.py:24
  16.4 182.9 %collective-permute-start.16 = (bf16[2,2,64,512]{3,2,1,0:T(8,128)(2,1)}, bf16[2,2,64,512]{3,2,1,0:T(8,128)(2,1)}, u32[]{:S(2)}, u32[]{:S(2)}) collective-permute-start(bf16[2,2,64,512]{3,2,1,0:T(8,128)(2,1)} %param.10), channel_id=1, source_target_pairs={{0,254},{2,0},{4,2},{6,4},{8,6},{10,8},{12,10},{14,12},{16,14},{18... | collective-permute-start | bytes 786440 | tf_op jit(solution)/shard_map/ppermute | solution.py:24
  27.1 40.5 %collective-permute-start = (bf16[2,2,2,64,256]{4,3,0,2,1:T(8,128)(2,1)S(1)}, bf16[2,2,2,64,256]{4,3,0,2,1:T(8,128)(2,1)S(1)}, u32[]{:S(2)}, u32[]{:S(2)}) collective-permute-start(bf16[2,2,2,64,256]{4,3,0,2,1:T(8,128)(2,1)S(1)} %bitcast.655), channel_id=1, source_target_pairs={{0,256},{256,0},{1,257},{257,1},{2,258},{258,2},{3,259},{259,3},{4... | collective-permute-start | bytes 786440 | tf_op jit(solution)/shard_map/ppermute | solution.py:19
  67.7 9.4 collective-permute-start.1
  77.0 9.9 collective-permute-start.2
  87.0 16.6 %collective-permute-start.3 = (bf16[2,2,2,64,256]{4,3,0,2,1:T(8,128)(2,1)S(1)}, bf16[2,2,2,64,256]{4,3,0,2,1:T(8,128)(2,1)S(1)}, u32[]{:S(2)}, u32[]{:S(2)}) collective-permute-start(bf16[2,2,2,64,256]{4,3,0,2,1:T(8,128)(2,1)S(1)} %collective-permute-done.2), channel_id=1, source_target_pairs={{0,8},{8,0},{2,10},{10,2},{4,12},{12,4},{6,14},{14,6},{16,24},{24,... | collective-permute-start | bytes 786440 | tf_op jit(solution)/shard_map/ppermute | solution.py:19
  103.5 32.8 %collective-permute-start.4 = (bf16[2,2,2,64,256]{4,3,0,2,1:T(8,128)(2,1)S(1)}, bf16[2,2,2,64,256]{4,3,0,2,1:T(8,128)(2,1)S(1)}, u32[]{:S(2)}, u32[]{:S(2)}) collective-permute-start(bf16[2,2,2,64,256]{4,3,0,2,1:T(8,128)(2,1)S(1)} %collective-permute-done.3), channel_id=1, source_target_pairs={{0,16},{16,0},{2,18},{18,2},{4,20},{20,4},{6,22},{22,6},{8,24},{24... | collective-permute-start | bytes 786440 | tf_op jit(solution)/shard_map/ppermute | solution.py:19
  136.3 22.8 %collective-permute-start.5 = (bf16[2,2,2,64,256]{4,3,0,2,1:T(8,128)(2,1)S(1)}, bf16[2,2,2,64,256]{4,3,0,2,1:T(8,128)(2,1)S(1)}, u32[]{:S(2)}, u32[]{:S(2)}) collective-permute-start(bf16[2,2,2,64,256]{4,3,0,2,1:T(8,128)(2,1)S(1)} %collective-permute-done.4), channel_id=1, source_target_pairs={{0,32},{32,0},{2,34},{34,2},{4,36},{36,4},{6,38},{38,6},{8,40},{40... | collective-permute-start | bytes 786440 | tf_op jit(solution)/shard_map/ppermute | solution.py:19
  159.1 9.2 collective-permute-start.6
  168.3 43.4 %collective-permute-start.7 = (bf16[2,2,2,64,256]{4,3,0,2,1:T(8,128)(2,1)}, bf16[2,2,2,64,256]{4,3,0,2,1:T(8,128)(2,1)}, u32[]{:S(2)}, u32[]{:S(2)}) collective-permute-start(bf16[2,2,2,64,256]{4,3,0,2,1:T(8,128)(2,1)} %collective-permute-done.6), channel_id=1, source_target_pairs={{0,128},{128,0},{2,130},{130,2},{4,132},{132,4},{6,134},{134,6},{8... | collective-permute-start | bytes 786440 | tf_op jit(solution)/shard_map/ppermute | solution.py:19
  197.2 730.0 %collective-permute-start.13 = (bf16[2,2,64,512]{3,2,1,0:T(8,128)(2,1)}, bf16[2,2,64,512]{3,2,1,0:T(8,128)(2,1)}, u32[]{:S(2)}, u32[]{:S(2)}) collective-permute-start(bf16[2,2,64,512]{3,2,1,0:T(8,128)(2,1)} %collective-permute-done.10), channel_id=1, source_target_pairs={{0,2},{2,4},{4,6},{6,8},{8,10},{10,12},{12,14},{14,16},{16,18},{18... | collective-permute-start | bytes 786440 | tf_op jit(solution)/shard_map/ppermute | solution.py:24
  199.2 740.5 %collective-permute-start.19 = (bf16[2,2,64,512]{3,2,1,0:T(8,128)(2,1)}, bf16[2,2,64,512]{3,2,1,0:T(8,128)(2,1)}, u32[]{:S(2)}, u32[]{:S(2)}) collective-permute-start(bf16[2,2,64,512]{3,2,1,0:T(8,128)(2,1)} %collective-permute-done.16), channel_id=1, source_target_pairs={{0,254},{2,0},{4,2},{6,4},{8,6},{10,8},{12,10},{14,12},{16,14},{18... | collective-permute-start | bytes 786440 | tf_op jit(solution)/shard_map/ppermute | solution.py:24
  202.8 714.9 %collective-permute-start.12 = (bf16[2,2,256,256]{3,2,1,0:T(8,128)(2,1)}, bf16[2,2,256,256]{3,2,1,0:T(8,128)(2,1)}, u32[]{:S(2)}, u32[]{:S(2)}) collective-permute-start(bf16[2,2,256,256]{3,2,1,0:T(8,128)(2,1)} %collective-permute-done.9), channel_id=1, source_target_pairs={{0,2},{2,4},{4,6},{6,8},{8,10},{10,12},{12,14},{14,16},{16,18},{18... | collective-permute-start | bytes 1572872 | tf_op jit(solution)/shard_map/ppermute | solution.py:24
  204.8 730.2 %collective-permute-start.18 = (bf16[2,2,256,256]{3,2,1,0:T(8,128)(2,1)}, bf16[2,2,256,256]{3,2,1,0:T(8,128)(2,1)}, u32[]{:S(2)}, u32[]{:S(2)}) collective-permute-start(bf16[2,2,256,256]{3,2,1,0:T(8,128)(2,1)} %collective-permute-done.15), channel_id=1, source_target_pairs={{0,254},{2,0},{4,2},{6,4},{8,6},{10,8},{12,10},{14,12},{16,14},{18... | collective-permute-start | bytes 1572872 | tf_op jit(solution)/shard_map/ppermute | solution.py:24
  216.0 667.9 %collective-permute-start.8 = (bf16[2,2,2,64,256]{4,3,0,2,1:T(8,128)(2,1)}, bf16[2,2,2,64,256]{4,3,0,2,1:T(8,128)(2,1)}, u32[]{:S(2)}, u32[]{:S(2)}) collective-permute-start(bf16[2,2,2,64,256]{4,3,0,2,1:T(8,128)(2,1)} %fusion.89), channel_id=1, source_target_pairs={{0,2},{2,4},{4,6},{6,8},{8,10},{10,12},{12,14},{14,16},{16,18},{18... | collective-permute-start | bytes 786440 | tf_op jit(solution)/shard_map/ppermute | solution.py:24
  223.1 657.9 %copy-start.46 = (bf16[2,2,64,256]{3,2,1,0:T(8,128)(2,1)S(1)}, bf16[2,2,64,256]{3,2,1,0:T(8,128)(2,1)}, u32[]{:S(2)}) copy-start(bf16[2,2,64,256]{3,2,1,0:T(8,128)(2,1)} %get-tuple-element.68) | copy-start | bytes 393220
  883.9 19.2 %collective-permute-start.14 = (bf16[2,2,2,64,256]{4,3,0,2,1:T(8,128)(2,1)}, bf16[2,2,2,64,256]{4,3,0,2,1:T(8,128)(2,1)S(1)}, u32[]{:S(2)}, u32[]{:S(2)}) collective-permute-start(bf16[2,2,2,64,256]{4,3,0,2,1:T(8,128)(2,1)} %fusion.89), channel_id=1, source_target_pairs={{0,254},{2,0},{4,2},{6,4},{8,6},{10,8},{12,10},{14,12},{16,14},{18... | collective-permute-start | bytes 786440 | tf_op jit(solution)/shard_map/ppermute | solution.py:24
  903.1 19.5 %collective-permute-start.11 = (bf16[2,2,2,64,256]{4,3,0,2,1:T(8,128)(2,1)}, bf16[2,2,2,64,256]{4,3,0,2,1:T(8,128)(2,1)S(1)}, u32[]{:S(2)}, u32[]{:S(2)}) collective-permute-start(bf16[2,2,2,64,256]{4,3,0,2,1:T(8,128)(2,1)} %collective-permute-done.8), channel_id=1, source_target_pairs={{0,2},{2,4},{4,6},{6,8},{8,10},{10,12},{12,14},{14,16},{16,18},{18... | collective-permute-start | bytes 786440 | tf_op jit(solution)/shard_map/ppermute | solution.py:24
  917.7 17.3 %collective-permute-start.17 = (bf16[2,2,2,64,256]{4,3,0,2,1:T(8,128)(2,1)S(1)}, bf16[2,2,2,64,256]{4,3,0,2,1:T(8,128)(2,1)S(1)}, u32[]{:S(2)}, u32[]{:S(2)}) collective-permute-start(bf16[2,2,2,64,256]{4,3,0,2,1:T(8,128)(2,1)S(1)} %collective-permute-done.14), channel_id=1, source_target_pairs={{0,254},{2,0},{4,2},{6,4},{8,6},{10,8},{12,10},{14,12},{16,14},{18... | collective-permute-start | bytes 786440 | tf_op jit(solution)/shard_map/ppermute | solution.py:24
  972.0 102.2 %copy-start.1 = (f32[512,256]{1,0:T(8,128)S(1)}, f32[512,256]{1,0:T(8,128)}, u32[]{:S(2)}) copy-start(f32[512,256]{1,0:T(8,128)} %param.13) | copy-start | bytes 1572868
  991.3 6.3 collective-permute-start.20
  997.6 4.4 collective-permute-start.21
  1002.0 6.6 collective-permute-start.22
  1008.6 10.0 collective-permute-start.23
  1018.6 17.8 %collective-permute-start.24 = (bf16[2,2,2,64,128]{4,3,0,2,1:T(8,128)(2,1)S(1)}, bf16[2,2,2,64,128]{4,3,0,2,1:T(8,128)(2,1)S(1)}, u32[]{:S(2)}, u32[]{:S(2)}) collective-permute-start(bf16[2,2,2,64,128]{4,3,0,2,1:T(8,128)(2,1)S(1)} %collective-permute-done.23), channel_id=1, source_target_pairs={{0,16},{16,0},{2,18},{18,2},{4,20},{20,4},{6,22},{22,6},{8,24},{24... | collective-permute-start | bytes 393224 | tf_op jit(solution)/shard_map/ppermute | solution.py:19
  1036.4 24.1 %collective-permute-start.25 = (bf16[2,2,2,64,128]{4,3,0,2,1:T(8,128)(2,1)S(1)}, bf16[2,2,2,64,128]{4,3,0,2,1:T(8,128)(2,1)S(1)}, u32[]{:S(2)}, u32[]{:S(2)}) collective-permute-start(bf16[2,2,2,64,128]{4,3,0,2,1:T(8,128)(2,1)S(1)} %collective-permute-done.24), channel_id=1, source_target_pairs={{0,32},{32,0},{2,34},{34,2},{4,36},{36,4},{6,38},{38,6},{8,40},{40... | collective-permute-start | bytes 393224 | tf_op jit(solution)/shard_map/ppermute | solution.py:19
  1060.5 5.7 collective-permute-start.26
  1066.2 7.2 collective-permute-start.27
  (58 other events, 509.3 us)
Sparse Core Ops, SparseCore 0:
  973.6 15.3 reduce-scatter.3

commit v2 on v0

v2 whole, which is shorter than its diff:
```python
import functools

import jax
import jax.numpy as jnp
from jax import lax
from jax.experimental import pallas as pl
from jax.experimental.pallas import tpu as pltpu
from jax.sharding import PartitionSpec as P

REACH = 2
KDEV = 2
SLOTS = 2 * REACH + 1
BF16 = jnp.bfloat16
F32 = jnp.float32
MESH = pl.DeviceIdType.MESH


def dot_nn(left, right):
    return lax.dot_general(left, right, (((1,), (0,)), ((), ())), preferred_element_type=F32)


def dot_nt(left, right, precision=None):
    return lax.dot_general(
        left, right, (((1,), (1,)), ((), ())), preferred_element_type=F32, precision=precision
    )


def kernel(
    grid,
    amps,
    cond_hbm,
    val_hbm,
    energy_hbm,
    screened_hbm,
    coulomb_hbm,
    mirror,
    classes,
    out,
    cond,
    vals,
    energy,
    screened,
    coulomb,
    xbuf,
    ybuf,
    gbuf,
    mbuf,
    sbuf,
    backs,
    fields,
    owns,
    rs_send,
    rs_recv,
    results,
    land_x,
    land_y,
    ar_a,
    ar_b,
    ar_c,
    rho_rows,
    u_send,
    u_recv,
    local_sem,
    send_sem,
    recv_sem,
):
    nx, nz_hi, nz_lo, nk = grid
    nz = nz_hi * nz_lo
    blocks = nx * nz * 2
    pm = lax.axis_index("pm")
    ka = lax.axis_index("ka")
    side = lax.axis_index("isdf")
    core = ka % 2
    z = (ka // 2) % nz
    x = ka // (2 * nz)
    z_lo, z_hi = z % nz_lo, z // nz_lo
    nv, nc = xbuf.shape[2], xbuf.shape[3]
    nmu = cond.shape[3]
    nnu = vals.shape[4]
    half = nc // 2

    mate = ka + 1 - 2 * core
    above = (ka + REACH) % blocks
    below = (ka + blocks - REACH) % blocks
    across = blocks - 1 - ka

    def ka_of(x_at, z_at, core_at):
        return (x_at * nz + z_at) * 2 + core_at

    a_size = 2 * nx
    a_index = x * 2 + core

    def a_peer(step):
        other = (a_index + step) % a_size
        return ka_of(other // 2, z, other % 2)

    def b_peer(step):
        return ka_of(x, z_hi * nz_lo + (z_lo + step) % nz_lo, core)

    def c_peer(step):
        return ka_of(x, ((z_hi + step) % nz_hi) * nz_lo + z_lo, core)

    here = {"pm": pm, "ka": ka, "isdf": side}

    def device(**change):
        return {**here, **change}

    counter = {"local": 0, "send": 0, "recv": 0}

    def take(kind, count=1):
        first = counter[kind]
        counter[kind] += count
        return first

    def local(src, dst):
        return pltpu.make_async_copy(src, dst, local_sem.at[take("local")])

    pending = []

    def remote(src, dst, recv, target):
        copy = pltpu.make_async_remote_copy(
            src_ref=src,
            dst_ref=dst,
            send_sem=send_sem.at[take("send")],
            recv_sem=recv_sem.at[recv],
            device_id=target,
            device_id_type=MESH,
        )
        return copy

    def launch(src, dst, recv, target):
        copy = remote(src, dst, recv, target)
        copy.start()
        pending.append(copy)

    def arrive(dst, recv):
        pltpu.make_async_remote_copy(
            src_ref=dst,
            dst_ref=dst,
            send_sem=send_sem.at[0],
            recv_sem=recv_sem.at[recv],
            device_id=device(isdf=1 - side),
            device_id_type=MESH,
        ).wait_recv()

    greeted = [
        device(pm=1 - pm),
        device(pm=0, ka=across),
        device(pm=1, ka=across),
        device(isdf=1 - side),
        device(ka=above),
        device(ka=below),
        device(ka=mate),
    ]
    greeted += [device(ka=a_peer(step)) for step in range(1, a_size)]
    greeted += [device(ka=b_peer(step)) for step in range(1, nz_lo)]
    greeted += [device(ka=c_peer(step)) for step in range(1, nz_hi)]
    barrier = pltpu.get_barrier_semaphore()
    for target in greeted:
        pl.semaphore_signal(barrier, inc=1, device_id=target, device_id_type=MESH)

    load_v = local(val_hbm, vals.at[REACH])
    load_c = local(cond_hbm, cond)
    load_x = local(amps.at[0, 0], xbuf)
    load_s = local(screened_hbm, screened)
    load_k = local(coulomb_hbm, coulomb)
    load_e = local(energy_hbm, energy)
    load_v.start()
    load_c.start()

    @pl.when(pm == 0)
    def _():
        load_x.start()

    load_s.start()
    load_k.start()
    load_e.start()
    pl.semaphore_wait(barrier, len(greeted))

    x_recv = take("recv")
    y_recv = take("recv")
    y_pass_recv = take("recv")
    v_recv = take("recv", SLOTS)
    g_recv = [take("recv", SLOTS) for _ in range(2)]
    send_x = remote(amps.at[0, 1], xbuf, x_recv, device(pm=1))
    send_y = [
        remote(amps.at[0, b, :, side], ybuf.at[:, side], y_recv, device(pm=b, ka=across)) for b in (1, 0)
    ]

    @pl.when(pm == 1)
    def _():
        for copy in send_y:
            copy.start()

    @pl.when(pm == 0)
    def _():
        send_x.start()

    mate_there = 1 + 2 * core
    mate_here = 3 - 2 * core
    pass_from = 4 - 4 * core
    pass_there = 3 - 2 * core
    passed_here = 1 + 2 * core
    direct_here = 4 * core

    def spread_block(block, landing, recv):
        launch(block, landing.at[0], recv, device(ka=above))
        launch(block, landing.at[SLOTS - 1], recv + SLOTS - 1, device(ka=below))
        launch(block, landing.at[mate_there], recv + mate_there, device(ka=mate))

    def pass_block(landing, recv):
        arrive(landing.at[pass_from], recv + pass_from)
        launch(landing.at[pass_from], landing.at[pass_there], recv + pass_there, device(ka=mate))

    spread_block(val_hbm, vals, v_recv)

    my_mu = pl.ds(pl.multiple_of(side * nmu, nmu), nmu)
    my_half = pl.ds(pl.multiple_of(side * half, half), half)

    def transform(channel, k, z_real, z_imag, sign):
        stack = jnp.concatenate([z_real, z_imag], axis=0)
        with_real = dot_nn(stack, cond[0, k])
        with_imag = dot_nn(stack, cond[1, k])
        g_real = with_real[:nv] - sign * with_imag[nv:]
        g_imag = with_imag[:nv] + sign * with_real[nv:]
        g_all = jnp.concatenate([g_real, g_imag], axis=0)
        gbuf[channel, REACH, k] = jnp.transpose(g_all).astype(BF16)
        v_real = vals[REACH, 0, k, :, my_mu].astype(F32)
        v_imag = vals[REACH, 1, k, :, my_mu].astype(F32)
        rho_real = jnp.sum(v_real * g_real + v_imag * g_imag, axis=0, keepdims=True)
        rho_imag = jnp.sum(v_real * g_imag - v_imag * g_real, axis=0, keepdims=True)
        return rho_real, rho_imag

    load_c.wait()
    load_v.wait()

    @pl.when(pm == 0)
    def _():
        load_x.wait()

    @pl.when(pm == 1)
    def _():
        arrive(xbuf, x_recv)

    rho_x = [transform(0, k, xbuf[0, k], xbuf[1, k], 1.0) for k in range(KDEV)]
    spread_block(gbuf.at[0, REACH], gbuf.at[0], g_recv[0])

    arrive(ybuf.at[:, side], y_recv)
    launch(ybuf.at[:, side], ybuf.at[:, side], y_pass_recv, device(isdf=1 - side))
    arrive(ybuf.at[:, 1 - side], y_pass_recv)
    mirrored = [lax.rem(mirror[k], KDEV) for k in range(KDEV)]
    rho_y = [transform(1, k, ybuf[0, mirrored[k]], ybuf[1, mirrored[k]], -1.0) for k in range(KDEV)]
    spread_block(gbuf.at[1, REACH], gbuf.at[1], g_recv[1])

    rho_real = sum(part[0] for part in rho_x + rho_y)
    rho_imag = sum(part[1] for part in rho_x + rho_y)
    lanes = 128
    pieces = nmu // lanes

    def put_rho(buffer, index, value):
        buffer[pl.ds(index, 1)] = value[None]

    rho_rows[...] = jnp.zeros_like(rho_rows)
    for piece in range(pieces):
        rho_rows[pl.ds(piece, 1), :] = rho_real[:, piece * lanes : (piece + 1) * lanes]
        rho_rows[pl.ds(pieces + piece, 1), :] = rho_imag[:, piece * lanes : (piece + 1) * lanes]

    def stage(buffer, index, size, peer, value):
        base = take("recv", size)
        put_rho(buffer, index, value)
        for step in range(1, size):
            launch(buffer.at[index], buffer.at[index], base + index, device(ka=peer(step)))
        return base

    def finish(buffer, index, size, base):
        for step in range(1, size):
            other = (index + step) % size
            arrive(buffer.at[other], base + other)
        return jnp.sum(buffer[...], axis=0)

    base_a = stage(ar_a, a_index, a_size, a_peer, rho_rows[...])

    def pairs(channel, slot):
        def one(k, carry):
            v_real = vals[slot, 0, k]
            v_imag = vals[slot, 1, k]
            coef = gbuf[channel, slot, k]
            at = slot * KDEV + k
            mbuf[at, 0] = dot_nn(coef, jnp.concatenate([v_real, v_imag], axis=0)).astype(BF16)
            mbuf[at, 1] = dot_nn(coef, jnp.concatenate([-v_imag, v_real], axis=0)).astype(BF16)
            return carry

        lax.fori_loop(0, KDEV, one, 0)

    shifts = SLOTS * KDEV + 1
    kinds = [classes[0, (ka * KDEV + nk - (e - SLOTS)) % nk] for e in range(shifts)]

    def screen():
        rows = 16

        def one(i, carry):
            row = pl.ds(pl.multiple_of(i * rows, rows), rows)
            for column in range(0, nnu, 128):
                col = pl.ds(column, 128)
                total = [[None, None] for _ in range(KDEV)]
                weights = [None] * shifts
                for e in range(shifts):
                    weights[e] = (screened[kinds[e], 0, row, col], screened[kinds[e], 1, row, col])
                for t in range(SLOTS * KDEV):
                    m_real = mbuf[t, 0, row, col]
                    m_imag = mbuf[t, 1, row, col]
                    for k in range(KDEV):
                        w_real, w_imag = weights[SLOTS * KDEV - 1 + k - t]
                        real = w_real * m_real - w_imag * m_imag
                        imag = w_real * m_imag + w_imag * m_real
                        old = total[k]
                        total[k] = [real, imag] if old[0] is None else [old[0] + real, old[1] + imag]
                for k in range(KDEV):
                    sbuf[k, 0, row, col] = total[k][0]
                    sbuf[k, 1, row, col] = total[k][1]
            return carry

        lax.fori_loop(0, nmu // rows, one, 0)

    def back(channel):
        for k in range(KDEV):
            stack = jnp.concatenate([vals[REACH, 0, k], vals[REACH, 1, k]], axis=0)
            with_real = dot_nt(stack, sbuf[k, 0])
            with_imag = dot_nt(stack, sbuf[k, 1])
            backs[channel, k, 0] = with_real[:nv] - with_imag[nv:]
            backs[channel, k, 1] = with_real[nv:] + with_imag[:nv]

    pairs(0, REACH)
    pass_block(vals, v_recv)
    pass_block(gbuf.at[0], g_recv[0])

    def wait_slot(landing, recv, slot):
        arrive(landing.at[slot], recv + slot)

    load_s.wait()
    for slot in (mate_here, pass_from, direct_here, passed_here):
        if slot is not pass_from:
            wait_slot(vals, v_recv, slot)
            wait_slot(gbuf.at[0], g_recv[0], slot)
        pairs(0, slot)
    base_b = stage(ar_b, z_lo, nz_lo, b_peer, finish(ar_a, a_index, a_size, base_a))
    screen()
    pass_block(gbuf.at[1], g_recv[1])
    base_c = stage(ar_c, z_hi, nz_hi, c_peer, finish(ar_b, z_lo, nz_lo, base_b))
    back(0)

    pairs(1, REACH)
    for slot in (mate_here, pass_from, direct_here, passed_here):
        if slot is not pass_from:
            wait_slot(gbuf.at[1], g_recv[1], slot)
        pairs(1, slot)

    rho = finish(ar_c, z_hi, nz_hi, base_c)
    load_k.wait()
    density = jnp.concatenate(
        [
            jnp.concatenate([rho[piece : piece + 1] for piece in range(pieces)], axis=1),
            jnp.concatenate([rho[pieces + piece : pieces + piece + 1] for piece in range(pieces)], axis=1),
            jnp.zeros((6, nmu), F32),
        ],
        axis=0,
    )
    spread = dot_nt(density, coulomb[...], lax.Precision.HIGHEST)
    first, second = spread[:, :nmu], spread[:, nmu:]
    u_own = jnp.where(side == 0, first, second)
    u_send[...] = jnp.where(side == 0, second, first)
    u_at = take("recv")
    launch(u_send, u_recv, u_at, device(isdf=1 - side))

    screen()
    back(1)

    arrive(u_recv, u_at)
    potential = u_own + u_recv[...]
    u_real, u_imag = 2.0 * potential[0:1], 2.0 * potential[1:2]
    rs_at = take("recv", 2 * KDEV)
    for k in range(KDEV):
        v_real = vals[REACH, 0, k, :, my_mu].astype(F32)
        v_imag = vals[REACH, 1, k, :, my_mu].astype(F32)
        exchange_real = u_real * v_real - u_imag * v_imag
        exchange_imag = u_real * v_imag + u_imag * v_real
        for channel in (1, 0):
            fields[channel, k] = jnp.concatenate(
                [exchange_real - backs[channel, k, 0], exchange_imag - backs[channel, k, 1]], axis=0
            ).astype(BF16)
            with_real = dot_nt(fields[channel, k], cond[0, k])
            with_imag = dot_nt(fields[channel, k], cond[1, k])
            for part, value in (
                (0, with_real[:nv] + with_imag[nv:]),
                (1, with_real[nv:] - with_imag[:nv]),
            ):
                owns[channel, k, part] = jnp.where(side == 0, value[:, :half], value[:, half:])
                rs_send[channel, k, part] = jnp.where(side == 0, value[:, half:], value[:, :half]).astype(BF16)
            at = channel * KDEV + k
            launch(rs_send.at[channel, k], rs_recv.at[channel, k], rs_at + at, device(isdf=1 - side))

    load_e.wait()
    land_at = take("recv", KDEV)
    land_x_at = take("recv", KDEV)
    cross_at = take("recv", 2 * KDEV)
    back_x = []
    for k in range(KDEV):
        for channel in (1, 0):
            arrive(rs_recv.at[channel, k], rs_at + channel * KDEV + k)
            for part in range(2):
                if channel == 0:
                    amp = xbuf[part, k, :, my_half].astype(F32)
                else:
                    amp = ybuf[part, mirrored[k], :, my_half].astype(F32)
                    amp = -amp if part == 1 else amp
                value = energy[k] * amp + owns[channel, k, part] + rs_recv[channel, k, part].astype(F32)
                if channel == 1 and part == 1:
                    value = -value
                results[channel, k, part] = value.astype(BF16)
            if channel == 1:
                launch(
                    results.at[1, k],
                    land_y.at[pm, k],
                    cross_at + pm * KDEV + k,
                    device(pm=1, ka=across),
                )
            else:
                back_x.append(remote(results.at[0, k], land_x.at[k], land_x_at + k, device(pm=0)))

                @pl.when(pm == 1)
                def _(copy=back_x[-1]):
                    copy.start()

    @pl.when(pm == 0)
    def _():
        for k in range(KDEV):
            out[0, 0, :, k] = results[0, k]
        for k in range(KDEV):
            arrive(land_x.at[k], land_x_at + k)
            out[0, 1, :, k] = land_x[k]

    @pl.when(pm == 1)
    def _():
        for b in range(2):
            for k in range(KDEV):
                arrive(land_y.at[b, k], cross_at + b * KDEV + k)
        for b in range(2):
            for k in range(KDEV):
                out[0, b, :, k] = land_y[b, mirrored[k]]

    for copy in pending:
        copy.wait_send()

    @pl.when(pm == 0)
    def _():
        send_x.wait_send()

    @pl.when(pm == 1)
    def _():
        for copy in send_y + back_x:
            copy.wait_send()


def per_device(grid, amplitudes, conduction, valence, energy, screened, coulomb, mirror, transfer_class):
    nx, nz_hi, nz_lo = grid[:3]
    _, vectors, _, _, nv, nc = amplitudes.shape
    nmu = conduction.shape[3]
    nnu = valence.shape[3]
    half = energy.shape[2]
    pair = (2, KDEV)
    hbm = pl.BlockSpec(memory_space=pl.ANY)
    smem = pl.BlockSpec(memory_space=pltpu.SMEM)
    vmem = pl.BlockSpec(memory_space=pltpu.VMEM)
    return pl.pallas_call(
        functools.partial(kernel, grid),
        out_shape=jax.ShapeDtypeStruct((1, vectors, 2, KDEV, nv, half), BF16),
        in_specs=[hbm] * 6 + [smem] * 2,
        out_specs=vmem,
        scratch_shapes=[
            pltpu.VMEM(conduction.shape, BF16),
            pltpu.VMEM((SLOTS,) + valence.shape, BF16),
            pltpu.VMEM(energy.shape, F32),
            pltpu.VMEM(screened.shape, BF16),
            pltpu.VMEM(coulomb.shape, F32),
            pltpu.VMEM((2, KDEV, nv, nc), BF16),
            pltpu.VMEM((2, KDEV, nv, nc), BF16),
            pltpu.VMEM((2, SLOTS, KDEV, nmu, 2 * nv), BF16),
            pltpu.VMEM((SLOTS * KDEV, 2, nmu, nnu), BF16),
            pltpu.VMEM((KDEV, 2, nmu, nnu), BF16),
            pltpu.VMEM((2, KDEV, 2, nv, nmu), F32),
            pltpu.VMEM((2, KDEV, 2 * nv, nmu), BF16),
            pltpu.VMEM((2, KDEV, 2, nv, half), F32),
            pltpu.VMEM((2, KDEV, 2, nv, half), BF16),
            pltpu.VMEM((2, KDEV, 2, nv, half), BF16),
            pltpu.VMEM((2, KDEV, 2, nv, half), BF16),
            pltpu.VMEM((KDEV, 2, nv, half), BF16),
            pltpu.VMEM((2, KDEV, 2, nv, half), BF16),
            pltpu.VMEM((2 * nx, 8, 128), F32),
            pltpu.VMEM((nz_lo, 8, 128), F32),
            pltpu.VMEM((nz_hi, 8, 128), F32),
            pltpu.VMEM((8, 128), F32),
            pltpu.VMEM((8, nmu), F32),
            pltpu.VMEM((8, nmu), F32),
            pltpu.SemaphoreType.DMA((6,)),
            pltpu.SemaphoreType.DMA((64,)),
            pltpu.SemaphoreType.DMA((64,)),
        ],
        compiler_params=pltpu.CompilerParams(
            collective_id=0, has_side_effects=True, vmem_limit_bytes=40 * 2**20
        ),
    )(amplitudes, conduction, valence, energy, screened, coulomb, mirror, transfer_class)


def solution(mesh):
    blocks = mesh.shape["ka"]
    nz_lo = 4 if blocks >= 128 else 2
    nz_hi = 4 if blocks >= 128 else 1
    nx = blocks // (2 * nz_lo * nz_hi)
    return jax.shard_map(
        functools.partial(per_device, (nx, nz_hi, nz_lo, KDEV * blocks)),
        mesh=mesh,
        in_specs=(
            P("pm", None, None, "ka", None, None),
            P(None, "ka", None, "isdf"),
            P(None, "ka", None, None),
            P("ka", None, "isdf"),
            P(None, None, "isdf", None),
            P(None, "isdf"),
            P("ka"),
            P("ka", None),
        ),
        out_specs=P("pm", None, None, "ka", None, "isdf"),
        check_vma=False,
    )
```

time: 1100 us -> 76.3 us (0.07); the launches traced: 1090 us -> 75.1 us
  blocking collectives: 656 us -> 0 us
  waiting for transfers between devices: 128 us -> 0 us
  starting transfers between devices: 115 us -> 0 us
  matrix products: 76.3 us -> 0 us
  Pallas kernels: 0 us -> 66.7 us
  other arithmetic: 56.6 us -> 0 us
  local copies, waits for them, and re-layouts: 38.9 us -> 8.4 us
  between operations: 14.8 us -> 0.02 us
    psum x1 -> x0, blocking collectives: 656 us -> none  [per_device(): spread = lax.psum(spread, ('ka', 'isdf'))]
    ppermute x28 -> x0, starting transfers between devices: 115 us -> none  [the longest x16 65.3 us: swapped(): return lax.ppermute(block, axis, route)]
    ppermute x28 -> x0, waiting for transfers between devices: 112 us -> none  [the longest x16 112 us: swapped(): return lax.ppermute(block, axis, route)]
    dot_general x59 -> x0, matrix products: 76.3 us -> none  [the longest x48 53.3 us: single(): jnp.einsum(pattern, first, second, preferred_element_type=jnp.float32)]
    pallas_call x0 -> x1, Pallas kernels: none -> 66.7 us  [per_device(): pl.pallas_call(functools.partial(kernel, grid), out_shape=jax.ShapeDtypeS...]
    mul x16 -> x0, other arithmetic: 33.2 us -> none  [the longest x10 21.7 us: accumulate(): screen_real * visit_real - screen_imag * visit_imag]
    mul x20 -> x0, local copies, waits for them, and re-layouts: 23.1 us -> none  [the longest x10 12.2 us: accumulate(): screen_real * visit_real - screen_imag * visit_imag]
    convert_element_type x6 -> x0, other arithmetic: 22.7 us -> none  [the longest x1 9.54 us: per_device(): sum_real = totals[0].astype(jnp.bfloat16)]
  transfers between devices with their start and end apart: 29 -> 0, of which waited for: 14 -> 0; matrix products, arithmetic and copies ran while one was open for 12% -> 0% of each run, Pallas kernels for 0% -> 0%
where the time goes in v2:
time: 76.3 us; the launch traced here: 75.1 us
  Pallas kernels  66.7 us (87%)
  local copies, waits for them, and re-layouts  8.4 us (11%)
    pallas_call x1, Pallas kernels, per_device(): pl.pallas_call(functools.partial(kernel, grid), out_shape=jax.ShapeDtypeS...  66.7 us
    unnamed x17, local copies, waits for them, and re-layouts  8.4 us

profile of v2, /device:TPU:25, one launch (start us, length us, event | category | flops | bytes accessed | tf_op | source)
XLA Modules:
  0.0 75.1 jit_solution(5179256382725520786)
XLA Ops:
  0.0 0.0 copy-start
  0.0 1.6 %copy-done = bf16[4,2,256,512]{3,2,1,0:T(8,128)(2,1)S(1)} copy-done((bf16[4,2,256,512]{3,2,1,0:T(8,128)(2,1)S(1)}, bf16[4,2,256,512]{3,2,1,0:T(8,128)(2,1)}, u32[]{:S(2)}) %copy-start) | copy-done | bytes 2097176
  1.6 0.0 copy-start.1
  1.6 1.0 %copy-done.1 = bf16[2,2,256,256]{3,2,1,0:T(8,128)(2,1)S(1)} copy-done((bf16[2,2,256,256]{3,2,1,0:T(8,128)(2,1)S(1)}, bf16[2,2,256,256]{3,2,1,0:T(8,128)(2,1)}, u32[]{:S(2)}) %copy-start.1) | copy-done | bytes 524312
  2.6 0.0 copy-start.2
  2.6 1.0 %copy-done.2 = f32[512,256]{1,0:T(8,128)S(1)} copy-done((f32[512,256]{1,0:T(8,128)S(1)}, f32[512,256]{1,0:T(8,128)}, u32[]{:S(2)}) %copy-start.2) | copy-done | bytes 524312
  3.7 0.0 copy-start.3
  3.7 0.9 %copy-done.3 = bf16[1,2,2,2,64,256]{5,4,3,2,1,0:T(8,128)(2,1)S(1)} copy-done((bf16[1,2,2,2,64,256]{5,4,3,2,1,0:T(8,128)(2,1)S(1)}, bf16[1,2,2,2,64,256]{5,4,3,2,1,0:T(8,128)(2,1)}, u32[]{:S(2)}) %copy-start.3) | copy-done | bytes 262168
  4.6 0.0 copy-start.4
  4.6 0.9 %copy-done.4 = bf16[2,2,64,512]{3,2,1,0:T(8,128)(2,1)S(1)} copy-done((bf16[2,2,64,512]{3,2,1,0:T(8,128)(2,1)S(1)}, bf16[2,2,64,512]{3,2,1,0:T(8,128)(2,1)}, u32[]{:S(2)}) %copy-start.4) | copy-done | bytes 262168
  5.6 0.0 copy-start.5
  5.6 0.8 %copy-done.5 = f32[2,64,128]{2,1,0:T(8,128)S(1)} copy-done((f32[2,64,128]{2,1,0:T(8,128)S(1)}, f32[2,64,128]{2,1,0:T(8,128)}, u32[]{:S(2)}) %copy-start.5) | copy-done | bytes 65560
  6.4 0.0 copy-start.6
  6.4 0.7 copy-done.6
  7.1 0.0 copy-start.7
  7.1 0.7 copy-done.7
  7.8 66.7 %shard_map.82 = bf16[1,2,2,2,64,128]{5,4,3,2,1,0:T(8,128)(2,1)S(1)} custom-call(bf16[1,2,2,2,64,256]{5,4,3,2,1,0:T(8,128)(2,1)S(1)} %copy-done.3, bf16[2,2,256,256]{3,2,1,0:T(8,128)(2,1)S(1)} %copy-done.1, bf16[2,2,64,512]{3,2,1,0:T(8,128)(2,1)S(1)} %copy-done.4, f32[2,64,128]{2,1,0:T(8,128)S(1)} %copy-done.5, bf16[4,2,256,512]{3,2,1,0:T(8,128)(2,1)S(1)} %copy-done, ...), custom_call_target="tpu_custom_call" | custom-call | tf_op jit(solution)/shard_map/pallas_call | solution.py:474
  74.4 0.7 copy.10
Async XLA Ops:
  0.0 1.6 %copy-start = (bf16[4,2,256,512]{3,2,1,0:T(8,128)(2,1)S(1)}, bf16[4,2,256,512]{3,2,1,0:T(8,128)(2,1)}, u32[]{:S(2)}) copy-start(bf16[4,2,256,512]{3,2,1,0:T(8,128)(2,1)} %screened_hbm.1) | copy-start | bytes 6291460
  1.6 1.0 %copy-start.1 = (bf16[2,2,256,256]{3,2,1,0:T(8,128)(2,1)S(1)}, bf16[2,2,256,256]{3,2,1,0:T(8,128)(2,1)}, u32[]{:S(2)}) copy-start(bf16[2,2,256,256]{3,2,1,0:T(8,128)(2,1)} %cond_hbm.1) | copy-start | bytes 1572868
  2.6 1.0 %copy-start.2 = (f32[512,256]{1,0:T(8,128)S(1)}, f32[512,256]{1,0:T(8,128)}, u32[]{:S(2)}) copy-start(f32[512,256]{1,0:T(8,128)} %coulomb_hbm.1) | copy-start | bytes 1572868
  3.7 0.9 %copy-start.3 = (bf16[1,2,2,2,64,256]{5,4,3,2,1,0:T(8,128)(2,1)S(1)}, bf16[1,2,2,2,64,256]{5,4,3,2,1,0:T(8,128)(2,1)}, u32[]{:S(2)}) copy-start(bf16[1,2,2,2,64,256]{5,4,3,2,1,0:T(8,128)(2,1)} %amps.1) | copy-start | bytes 786436
  4.6 0.9 %copy-start.4 = (bf16[2,2,64,512]{3,2,1,0:T(8,128)(2,1)S(1)}, bf16[2,2,64,512]{3,2,1,0:T(8,128)(2,1)}, u32[]{:S(2)}) copy-start(bf16[2,2,64,512]{3,2,1,0:T(8,128)(2,1)} %val_hbm.1) | copy-start | bytes 786436
  5.6 0.8 %copy-start.5 = (f32[2,64,128]{2,1,0:T(8,128)S(1)}, f32[2,64,128]{2,1,0:T(8,128)}, u32[]{:S(2)}) copy-start(f32[2,64,128]{2,1,0:T(8,128)} %energy_hbm.1) | copy-start | bytes 196612
  6.4 0.7 copy-start.6
  7.1 0.7 copy-start.7

commit v3 on v2

v3 whole, which is shorter than its diff:
```python
import functools

import jax
import jax.numpy as jnp
from jax import lax
from jax.experimental import pallas as pl
from jax.experimental.pallas import tpu as pltpu
from jax.sharding import PartitionSpec as P

REACH = 2
KDEV = 2
SLOTS = 2 * REACH + 1
BF16 = jnp.bfloat16
F32 = jnp.float32
MESH = pl.DeviceIdType.MESH


def dot_nn(left, right):
    return lax.dot_general(left, right, (((1,), (0,)), ((), ())), preferred_element_type=F32)


def dot_nt(left, right, precision=None):
    return lax.dot_general(
        left, right, (((1,), (1,)), ((), ())), preferred_element_type=F32, precision=precision
    )


def kernel(
    grid,
    amps,
    cond_hbm,
    val_hbm,
    energy_hbm,
    screened_hbm,
    coulomb_hbm,
    mirror,
    classes,
    out,
    cond,
    vals,
    energy,
    screened,
    coulomb,
    xbuf,
    ybuf,
    yhop,
    gbuf,
    mbuf,
    sbuf,
    backs,
    owns,
    rs_send,
    rs_recv,
    results,
    land_x,
    land_y,
    coulomb_high,
    coulomb_low,
    ar_out,
    ar_a,
    ar_b,
    local_sem,
    send_sem,
    recv_sem,
):
    nx, nz, nk = grid
    blocks = nx * nz * 2
    pm = lax.axis_index("pm")
    ka = lax.axis_index("ka")
    side = lax.axis_index("isdf")
    core = ka % 2
    z = (ka // 2) % nz
    x = ka // (2 * nz)
    nv, nc = xbuf.shape[2], xbuf.shape[3]
    nmu = cond.shape[3]
    nnu = vals.shape[4]
    half = nc // 2

    mate = ka + 1 - 2 * core
    above = (ka + REACH) % blocks
    below = (ka + blocks - REACH) % blocks
    across = blocks - 1 - ka

    def ka_of(x_at, z_at, core_at):
        return (x_at * nz + z_at) * 2 + core_at

    a_size = 4 * nx
    a_index = (x * 2 + core) * 2 + side

    def a_peer(step):
        other = (a_index + step) % a_size
        return {"ka": ka_of(other // 4, z, (other // 2) % 2), "isdf": other % 2}

    def b_peer(step):
        return {"ka": ka_of(x, (z + step) % nz, core)}

    here = {"pm": pm, "ka": ka, "isdf": side}

    def device(**change):
        return {**here, **change}

    counter = {"local": 0, "send": 0, "recv": 0}

    def take(kind, count=1):
        first = counter[kind]
        counter[kind] += count
        return first

    def local(src, dst):
        return pltpu.make_async_copy(src, dst, local_sem.at[take("local")])

    pending = []

    def remote(src, dst, recv, target):
        copy = pltpu.make_async_remote_copy(
            src_ref=src,
            dst_ref=dst,
            send_sem=send_sem.at[take("send")],
            recv_sem=recv_sem.at[recv],
            device_id=target,
            device_id_type=MESH,
        )
        return copy

    def launch(src, dst, recv, target):
        copy = remote(src, dst, recv, target)
        copy.start()
        pending.append(copy)

    def arrive(dst, recv):
        pltpu.make_async_remote_copy(
            src_ref=dst,
            dst_ref=dst,
            send_sem=send_sem.at[0],
            recv_sem=recv_sem.at[recv],
            device_id=device(isdf=1 - side),
            device_id_type=MESH,
        ).wait_recv()

    greeted = [
        device(pm=1 - pm),
        device(pm=0, ka=across),
        device(pm=1, ka=across),
        device(isdf=1 - side),
        device(ka=above),
        device(ka=below),
        device(ka=mate),
    ]
    greeted += [device(**a_peer(step)) for step in range(1, a_size)]
    greeted += [device(**b_peer(step)) for step in range(1, nz)]
    barrier = pltpu.get_barrier_semaphore()
    for target in greeted:
        pl.semaphore_signal(barrier, inc=1, device_id=target, device_id_type=MESH)

    load_v = local(val_hbm, vals.at[REACH])
    load_c = local(cond_hbm, cond)
    load_x = local(amps.at[0, 0], xbuf)
    load_s = local(screened_hbm, screened)
    load_k = local(coulomb_hbm, coulomb)
    load_e = local(energy_hbm, energy)
    load_v.start()
    load_c.start()

    @pl.when(pm == 0)
    def _():
        load_x.start()

    load_s.start()
    load_k.start()
    load_e.start()
    pl.semaphore_wait(barrier, len(greeted))

    x_recv = take("recv")
    hop_recv = take("recv", 2)
    y_recv = take("recv", 2)
    y_pass_recv = take("recv", 2)
    v_recv = take("recv", SLOTS)
    g_recv = [take("recv", SLOTS) for _ in range(2)]
    send_x = remote(amps.at[0, 1], xbuf, x_recv, device(pm=1))
    send_hop = [remote(amps.at[0, 0, part, side], yhop.at[part], hop_recv + part, device(pm=0)) for part in range(2)]
    send_y = [
        remote(amps.at[0, 1, part, side], ybuf.at[part, side], y_recv + part, device(ka=across))
        for part in range(2)
    ]
    pass_y = [remote(yhop.at[part], ybuf.at[part, side], y_recv + part, device(ka=across)) for part in range(2)]

    @pl.when(pm == 1)
    def _():
        for part in range(2):
            send_hop[part].start()
            send_y[part].start()

    @pl.when(pm == 0)
    def _():
        send_x.start()
        for part in range(2):
            arrive(yhop.at[part], hop_recv + part)
            pass_y[part].start()

    mate_there = 1 + 2 * core
    mate_here = 3 - 2 * core
    pass_from = 4 - 4 * core
    pass_there = 3 - 2 * core
    passed_here = 1 + 2 * core
    direct_here = 4 * core

    def spread_block(block, landing, recv):
        launch(block, landing.at[0], recv, device(ka=above))
        launch(block, landing.at[SLOTS - 1], recv + SLOTS - 1, device(ka=below))
        launch(block, landing.at[mate_there], recv + mate_there, device(ka=mate))

    def pass_block(landing, recv):
        arrive(landing.at[pass_from], recv + pass_from)
        launch(landing.at[pass_from], landing.at[pass_there], recv + pass_there, device(ka=mate))

    my_mu = pl.ds(pl.multiple_of(side * nmu, nmu), nmu)
    my_half = pl.ds(pl.multiple_of(side * half, half), half)

    def transform(channel, k, z_real, z_imag, sign):
        stack = jnp.concatenate([z_real, z_imag], axis=0)
        with_real = dot_nn(stack, cond[0, k])
        with_imag = dot_nn(stack, cond[1, k])
        g_real = with_real[:nv] - sign * with_imag[nv:]
        g_imag = with_imag[:nv] + sign * with_real[nv:]
        g_all = jnp.concatenate([g_real, g_imag], axis=0)
        gbuf[channel, REACH, k] = jnp.transpose(g_all).astype(BF16)
        v_real = vals[REACH, 0, k, :, my_mu].astype(F32)
        v_imag = vals[REACH, 1, k, :, my_mu].astype(F32)
        rho_real = jnp.sum(v_real * g_real + v_imag * g_imag, axis=0, keepdims=True)
        rho_imag = jnp.sum(v_real * g_imag - v_imag * g_real, axis=0, keepdims=True)
        return rho_real, rho_imag

    def pairs(channel, slot):
        def one(k, carry):
            v_real = vals[slot, 0, k]
            v_imag = vals[slot, 1, k]
            coef = gbuf[channel, slot, k]
            at = slot * KDEV + k
            mbuf[at, 0] = dot_nn(coef, jnp.concatenate([v_real, v_imag], axis=0)).astype(BF16)
            mbuf[at, 1] = dot_nn(coef, jnp.concatenate([-v_imag, v_real], axis=0)).astype(BF16)
            return carry

        lax.fori_loop(0, KDEV, one, 0)

    load_c.wait()
    load_v.wait()

    @pl.when(pm == 0)
    def _():
        load_x.wait()

    @pl.when(pm == 1)
    def _():
        arrive(xbuf, x_recv)

    spread_block(val_hbm, vals, v_recv)
    rho_x = [transform(0, k, xbuf[0, k], xbuf[1, k], 1.0) for k in range(KDEV)]
    spread_block(gbuf.at[0, REACH], gbuf.at[0], g_recv[0])

    def wait_slot(landing, recv, slot):
        arrive(landing.at[slot], recv + slot)

    late = (pass_from, direct_here, passed_here)

    def gather(channel, slots):
        for slot in slots:
            if slot is pass_from:
                if channel == 0:
                    pass_block(vals, v_recv)
                pass_block(gbuf.at[channel], g_recv[channel])
            else:
                if channel == 0:
                    wait_slot(vals, v_recv, slot)
                wait_slot(gbuf.at[channel], g_recv[channel], slot)
            pairs(channel, slot)

    pairs(0, REACH)
    load_k.wait()
    coulomb_high[...] = coulomb[...].astype(BF16)
    coulomb_low[...] = (coulomb[...] - coulomb[...].astype(BF16).astype(F32)).astype(BF16)
    gather(0, (mate_here,))
    for part in range(2):
        arrive(ybuf.at[part, side], y_recv + part)
        launch(ybuf.at[part, side], ybuf.at[part, side], y_pass_recv + part, device(isdf=1 - side))
    for part in range(2):
        arrive(ybuf.at[part, 1 - side], y_pass_recv + part)
    mirrored = [lax.rem(mirror[k], KDEV) for k in range(KDEV)]
    rho_y = [transform(1, k, ybuf[0, mirrored[k]], ybuf[1, mirrored[k]], -1.0) for k in range(KDEV)]
    spread_block(gbuf.at[1, REACH], gbuf.at[1], g_recv[1])

    density = jnp.concatenate(
        [
            sum(part[0] for part in rho_x + rho_y),
            sum(part[1] for part in rho_x + rho_y),
            jnp.zeros((6, nmu), F32),
        ],
        axis=0,
    )
    rest = density - density.astype(BF16).astype(F32)
    both = dot_nt(jnp.concatenate([density, rest], axis=0).astype(BF16), coulomb_high[...])
    share = both[:8] + both[8:] + dot_nt(density.astype(BF16), coulomb_low[...])
    lanes = 128
    pieces = nmu // lanes
    for there in range(2):
        for part in range(2):
            for piece in range(pieces):
                column = there * nmu + piece * lanes
                row = part * pieces + piece
                ar_out[there, pl.ds(row, 1), :] = share[part : part + 1, column : column + lanes]
    a_at = take("recv", a_size)
    for step in range(1, a_size):
        peer = a_peer(step)
        launch(ar_out.at[peer["isdf"]], ar_a.at[a_index], a_at + a_index, device(**peer))
    ar_a[a_index] = ar_out[side]
    b_at = take("recv", nz)

    def second_stage():
        for step in range(1, a_size):
            other = (a_index + step) % a_size
            arrive(ar_a.at[other], a_at + other)
        ar_b[z] = jnp.sum(ar_a[...], axis=0)
        for step in range(1, nz):
            launch(ar_b.at[z], ar_b.at[z], b_at + z, device(**b_peer(step)))

    def last_stage():
        for step in range(1, nz):
            other = (z + step) % nz
            arrive(ar_b.at[other], b_at + other)
        total = 2.0 * jnp.sum(ar_b[...], axis=0)
        return [
            jnp.concatenate([total[part * pieces + i : part * pieces + i + 1] for i in range(pieces)], axis=1)
            for part in range(2)
        ]

    shifts = SLOTS * KDEV + 1
    kinds = [classes[0, (ka * KDEV + nk - (e - SLOTS)) % nk] for e in range(shifts)]

    def screen(k):
        rows = 16

        def one(i, carry):
            row = pl.ds(pl.multiple_of(i * rows, rows), rows)
            for column in range(0, nnu, 128):
                col = pl.ds(column, 128)
                straight = crossed = turned = None
                for t in range(SLOTS * KDEV):
                    kind = kinds[SLOTS * KDEV - 1 + k - t]
                    w_real, w_imag = screened[kind, 0, row, col], screened[kind, 1, row, col]
                    m_real, m_imag = mbuf[t, 0, row, col], mbuf[t, 1, row, col]
                    first, second = w_real * m_real, w_imag * m_imag
                    mixed = w_real * m_imag + w_imag * m_real
                    straight = first if straight is None else straight + first
                    crossed = second if crossed is None else crossed + second
                    turned = mixed if turned is None else turned + mixed
                sbuf[k, 0, row, col] = straight - crossed
                sbuf[k, 1, row, col] = turned
            return carry

        lax.fori_loop(0, nmu // rows, one, 0)

    def back(channel, k):
        v_real, v_imag = vals[REACH, 0, k], vals[REACH, 1, k]
        summed = dot_nt(sbuf[k, 0], jnp.concatenate([v_real, v_imag], axis=0))
        summed = summed + dot_nt(sbuf[k, 1], jnp.concatenate([-v_imag, v_real], axis=0))
        backs[channel, k] = jnp.transpose(summed)

    gather(0, late)
    load_s.wait()
    screen(0)
    back(0, 0)
    second_stage()
    screen(1)
    back(0, 1)

    rs_at = take("recv", 2 * KDEV)
    land_x_at = take("recv", KDEV)
    cross_at = take("recv", 2 * KDEV)
    back_x = []

    def produce(channel, k, u_real, u_imag):
        v_real = vals[REACH, 0, k, :, my_mu].astype(F32)
        v_imag = vals[REACH, 1, k, :, my_mu].astype(F32)
        exchange = jnp.concatenate([u_real * v_real - u_imag * v_imag, u_real * v_imag + u_imag * v_real], axis=0)
        field = (exchange - backs[channel, k]).astype(BF16)
        with_real = dot_nt(field, cond[0, k])
        with_imag = dot_nt(field, cond[1, k])
        for part, value in (
            (0, with_real[:nv] + with_imag[nv:]),
            (1, with_real[nv:] - with_imag[:nv]),
        ):
            owns[channel, k, part] = jnp.where(side == 0, value[:, :half], value[:, half:])
            rs_send[channel, k, part] = jnp.where(side == 0, value[:, half:], value[:, :half]).astype(BF16)
        at = channel * KDEV + k
        launch(rs_send.at[channel, k], rs_recv.at[channel, k], rs_at + at, device(isdf=1 - side))

    def complete(channel, k):
        arrive(rs_recv.at[channel, k], rs_at + channel * KDEV + k)
        for part in range(2):
            if channel == 0:
                amp = xbuf[part, k, :, my_half].astype(F32)
            else:
                amp = ybuf[part, mirrored[k], :, my_half].astype(F32)
                amp = -amp if part == 1 else amp
            value = energy[k] * amp + owns[channel, k, part] + rs_recv[channel, k, part].astype(F32)
            if channel == 1 and part == 1:
                value = -value
            results[channel, k, part] = value.astype(BF16)
        if channel == 1:
            launch(results.at[1, k], land_y.at[pm, k], cross_at + pm * KDEV + k, device(pm=1, ka=across))
        else:
            copy = remote(results.at[0, k], land_x.at[k], land_x_at + k, device(pm=0))
            back_x.append(copy)

            @pl.when(pm == 1)
            def _():
                copy.start()

    pairs(1, REACH)
    gather(1, (mate_here,) + late)
    u_real, u_imag = last_stage()
    produce(0, 0, u_real, u_imag)
    produce(0, 1, u_real, u_imag)
    screen(0)
    back(1, 0)
    produce(1, 0, u_real, u_imag)
    screen(1)
    back(1, 1)
    load_e.wait()
    complete(1, 0)
    produce(1, 1, u_real, u_imag)
    complete(0, 0)
    complete(0, 1)
    complete(1, 1)

    @pl.when(pm == 0)
    def _():
        for k in range(KDEV):
            out[0, 0, :, k] = results[0, k]
        for k in range(KDEV):
            arrive(land_x.at[k], land_x_at + k)
            out[0, 1, :, k] = land_x[k]

    @pl.when(pm == 1)
    def _():
        for b in range(2):
            for k in range(KDEV):
                arrive(land_y.at[b, k], cross_at + b * KDEV + k)
        for b in range(2):
            for k in range(KDEV):
                out[0, b, :, k] = land_y[b, mirrored[k]]

    for copy in pending:
        copy.wait_send()

    @pl.when(pm == 0)
    def _():
        for copy in [send_x] + pass_y:
            copy.wait_send()

    @pl.when(pm == 1)
    def _():
        for copy in send_hop + send_y + back_x:
            copy.wait_send()


def per_device(grid, amplitudes, conduction, valence, energy, screened, coulomb, mirror, transfer_class):
    nx, nz = grid[:2]
    _, vectors, _, _, nv, nc = amplitudes.shape
    nmu = conduction.shape[3]
    nnu = valence.shape[3]
    half = energy.shape[2]
    pair = (2, KDEV)
    hbm = pl.BlockSpec(memory_space=pl.ANY)
    smem = pl.BlockSpec(memory_space=pltpu.SMEM)
    vmem = pl.BlockSpec(memory_space=pltpu.VMEM)
    return pl.pallas_call(
        functools.partial(kernel, grid),
        out_shape=jax.ShapeDtypeStruct((1, vectors, 2, KDEV, nv, half), BF16),
        in_specs=[hbm] * 6 + [smem] * 2,
        out_specs=vmem,
        scratch_shapes=[
            pltpu.VMEM(conduction.shape, BF16),
            pltpu.VMEM((SLOTS,) + valence.shape, BF16),
            pltpu.VMEM(energy.shape, F32),
            pltpu.VMEM(screened.shape, BF16),
            pltpu.VMEM(coulomb.shape, F32),
            pltpu.VMEM((2, KDEV, nv, nc), BF16),
            pltpu.VMEM((2, KDEV, nv, nc), BF16),
            pltpu.VMEM((2, nv, nc), BF16),
            pltpu.VMEM((2, SLOTS, KDEV, nmu, 2 * nv), BF16),
            pltpu.VMEM((SLOTS * KDEV, 2, nmu, nnu), BF16),
            pltpu.VMEM((KDEV, 2, nmu, nnu), BF16),
            pltpu.VMEM((2, KDEV, 2 * nv, nmu), F32),
            pltpu.VMEM((2, KDEV, 2, nv, half), F32),
            pltpu.VMEM((2, KDEV, 2, nv, half), BF16),
            pltpu.VMEM((2, KDEV, 2, nv, half), BF16),
            pltpu.VMEM((2, KDEV, 2, nv, half), BF16),
            pltpu.VMEM((KDEV, 2, nv, half), BF16),
            pltpu.VMEM((2, KDEV, 2, nv, half), BF16),
            pltpu.VMEM(coulomb.shape, BF16),
            pltpu.VMEM(coulomb.shape, BF16),
            pltpu.VMEM((2, 2 * nmu // 128, 128), F32),
            pltpu.VMEM((4 * nx, 2 * nmu // 128, 128), F32),
            pltpu.VMEM((nz, 2 * nmu // 128, 128), F32),
            pltpu.SemaphoreType.DMA((6,)),
            pltpu.SemaphoreType.DMA((80,)),
            pltpu.SemaphoreType.DMA((80,)),
        ],
        compiler_params=pltpu.CompilerParams(
            collective_id=0, has_side_effects=True, vmem_limit_bytes=60 * 2**20
        ),
    )(amplitudes, conduction, valence, energy, screened, coulomb, mirror, transfer_class)


def solution(mesh):
    blocks = mesh.shape["ka"]
    nz = 16 if blocks >= 128 else blocks // 4
    nx = blocks // (2 * nz)
    return jax.shard_map(
        functools.partial(per_device, (nx, nz, KDEV * blocks)),
        mesh=mesh,
        in_specs=(
            P("pm", None, None, "ka", None, None),
            P(None, "ka", None, "isdf"),
            P(None, "ka", None, None),
            P("ka", None, "isdf"),
            P(None, None, "isdf", None),
            P(None, "isdf"),
            P("ka"),
            P("ka", None),
        ),
        out_specs=P("pm", None, None, "ka", None, "isdf"),
        check_vma=False,
    )
```

time: 76.3 us -> 67.4 us (0.88)
  local copies, waits for them, and re-layouts: 8.4 us -> 1.57 us
  Pallas kernels: 66.7 us -> 64.8 us
    unnamed x17 -> x1, local copies, waits for them, and re-layouts: 8.4 us -> 1.57 us
    pallas_call x1, Pallas kernels: 66.7 us -> 64.8 us  [per_device(): pl.pallas_call(functools.partial(kernel, grid), out_shape=jax.ShapeDtypeS...]
where the time goes in v3:
time: 67.4 us; the launch traced here: 66.3 us
  Pallas kernels  64.8 us (96%)
  local copies, waits for them, and re-layouts  1.57 us (2%)
    pallas_call x1, Pallas kernels, per_device(): pl.pallas_call(functools.partial(kernel, grid), out_shape=jax.ShapeDtypeS...  64.8 us
    unnamed x1, local copies, waits for them, and re-layouts  1.57 us

profile of v3, /device:TPU:25, one launch (start us, length us, event | category | flops | bytes accessed | tf_op | source)
XLA Modules:
  0.0 66.3 jit_solution(12545377174571213711)
XLA Ops:
  0.0 64.8 %shard_map.82 = bf16[1,2,2,2,64,128]{5,4,3,2,1,0:T(8,128)(2,1)} custom-call(bf16[1,2,2,2,64,256]{5,4,3,2,1,0:T(8,128)(2,1)} %amps.1, bf16[2,2,256,256]{3,2,1,0:T(8,128)(2,1)} %cond_hbm.1, bf16[2,2,64,512]{3,2,1,0:T(8,128)(2,1)} %val_hbm.1, f32[2,64,128]{2,1,0:T(8,128)} %energy_hbm.1, bf16[4,2,256,512]{3,2,1,0:T(8,128)(2,1)} %screened_hbm.1, ...), custom_call_target="tpu_custom_call" | custom-call | tf_op jit(solution)/shard_map/pallas_call | solution.py:476
  64.8 1.6 %copy.10 = bf16[1,2,2,2,64,128]{5,4,3,2,1,0:T(8,128)(2,1)} copy(bf16[1,2,2,2,64,128]{5,4,3,2,1,0:T(8,128)(2,1)} %shard_map.82) | data formatting | bytes 262144

commit v4 on v3

--- a/solution.py
+++ b/solution.py
@@ -175,7 +175,7 @@
     y_recv = take("recv", 2)
     y_pass_recv = take("recv", 2)
     v_recv = take("recv", SLOTS)
-    g_recv = [take("recv", SLOTS) for _ in range(2)]
+    g_recv = [take("recv", SLOTS) for _ in range(1 + KDEV)]
     send_x = remote(amps.at[0, 1], xbuf, x_recv, device(pm=1))
     send_hop = [remote(amps.at[0, 0, part, side], yhop.at[part], hop_recv + part, device(pm=0)) for part in range(2)]
     send_y = [
@@ -193,9 +193,6 @@
     @pl.when(pm == 0)
     def _():
         send_x.start()
-        for part in range(2):
-            arrive(yhop.at[part], hop_recv + part)
-            pass_y[part].start()
 
     mate_there = 1 + 2 * core
     mate_here = 3 - 2 * core
@@ -253,25 +250,76 @@
     def _():
         arrive(xbuf, x_recv)
 
+    rho_x = [transform(0, k, xbuf[0, k], xbuf[1, k], 1.0) for k in range(KDEV)]
+
+    @pl.when(pm == 0)
+    def _():
+        for part in range(2):
+            arrive(yhop.at[part], hop_recv + part)
+            pass_y[part].start()
+
     spread_block(val_hbm, vals, v_recv)
-    rho_x = [transform(0, k, xbuf[0, k], xbuf[1, k], 1.0) for k in range(KDEV)]
     spread_block(gbuf.at[0, REACH], gbuf.at[0], g_recv[0])
+    forwards = [
+        remote(ybuf.at[part, side], ybuf.at[part, side], y_pass_recv + part, device(isdf=1 - side))
+        for part in range(2)
+    ]
+    pending.extend(forwards)
+
+    def forward_y():
+        for part in range(2):
+            arrive(ybuf.at[part, side], y_recv + part)
+            forwards[part].start()
+
+    @pl.when(pm == 1)
+    def _():
+        forward_y()
+
 
     def wait_slot(landing, recv, slot):
         arrive(landing.at[slot], recv + slot)
 
+    def screen(k, slots, fresh):
+        rows = 16
+        terms = []
+        for slot in slots:
+            for visitor in range(KDEV):
+                at = slot * KDEV + visitor
+                terms.append((at, classes[0, (ka * KDEV + nk - (SLOTS - 1) - k + at) % nk]))
+
+        def one(i, carry):
+            row = pl.ds(pl.multiple_of(i * rows, rows), rows)
+            for column in range(0, nnu, 128):
+                col = pl.ds(column, 128)
+                straight = None if fresh else sbuf[k, 0, row, col]
+                turned = None if fresh else sbuf[k, 1, row, col]
+                crossed = None
+                for at, kind in terms:
+                    w_real, w_imag = screened[kind, 0, row, col], screened[kind, 1, row, col]
+                    m_real, m_imag = mbuf[at, 0, row, col], mbuf[at, 1, row, col]
+                    first, second = w_real * m_real, w_imag * m_imag
+                    mixed = w_real * m_imag + w_imag * m_real
+                    straight = first if straight is None else straight + first
+                    crossed = second if crossed is None else crossed + second
+                    turned = mixed if turned is None else turned + mixed
+                sbuf[k, 0, row, col] = straight - crossed
+                sbuf[k, 1, row, col] = turned
+            return carry
+
+        lax.fori_loop(0, nmu // rows, one, 0)
+
     late = (pass_from, direct_here, passed_here)
 
     def gather(channel, slots):
+        flows = [(gbuf.at[1, :, k], g_recv[1 + k]) for k in range(KDEV)]
+        if channel == 0:
+            flows = [(vals, v_recv), (gbuf.at[0], g_recv[0])]
         for slot in slots:
-            if slot is pass_from:
-                if channel == 0:
-                    pass_block(vals, v_recv)
-                pass_block(gbuf.at[channel], g_recv[channel])
-            else:
-                if channel == 0:
-                    wait_slot(vals, v_recv, slot)
-                wait_slot(gbuf.at[channel], g_recv[channel], slot)
+            for landing, recv in flows:
+                if slot is pass_from:
+                    pass_block(landing, recv)
+                else:
+                    wait_slot(landing, recv, slot)
             pairs(channel, slot)
 
     pairs(0, REACH)
@@ -279,14 +327,21 @@
     coulomb_high[...] = coulomb[...].astype(BF16)
     coulomb_low[...] = (coulomb[...] - coulomb[...].astype(BF16).astype(F32)).astype(BF16)
     gather(0, (mate_here,))
-    for part in range(2):
-        arrive(ybuf.at[part, side], y_recv + part)
-        launch(ybuf.at[part, side], ybuf.at[part, side], y_pass_recv + part, device(isdf=1 - side))
+    load_s.wait()
+    for k in range(KDEV):
+        screen(k, (REACH, mate_here), True)
+
+    @pl.when(pm == 0)
+    def _():
+        forward_y()
+
     for part in range(2):
         arrive(ybuf.at[part, 1 - side], y_pass_recv + part)
     mirrored = [lax.rem(mirror[k], KDEV) for k in range(KDEV)]
-    rho_y = [transform(1, k, ybuf[0, mirrored[k]], ybuf[1, mirrored[k]], -1.0) for k in range(KDEV)]
-    spread_block(gbuf.at[1, REACH], gbuf.at[1], g_recv[1])
+    rho_y = []
+    for k in range(KDEV):
+        rho_y.append(transform(1, k, ybuf[0, mirrored[k]], ybuf[1, mirrored[k]], -1.0))
+        spread_block(gbuf.at[1, REACH, k], gbuf.at[1, :, k], g_recv[1 + k])
 
     density = jnp.concatenate(
         [
@@ -332,32 +387,6 @@
             for part in range(2)
         ]
 
-    shifts = SLOTS * KDEV + 1
-    kinds = [classes[0, (ka * KDEV + nk - (e - SLOTS)) % nk] for e in range(shifts)]
-
-    def screen(k):
-        rows = 16
-
-        def one(i, carry):
-            row = pl.ds(pl.multiple_of(i * rows, rows), rows)
-            for column in range(0, nnu, 128):
-                col = pl.ds(column, 128)
-                straight = crossed = turned = None
-                for t in range(SLOTS * KDEV):
-                    kind = kinds[SLOTS * KDEV - 1 + k - t]
-                    w_real, w_imag = screened[kind, 0, row, col], screened[kind, 1, row, col]
-                    m_real, m_imag = mbuf[t, 0, row, col], mbuf[t, 1, row, col]
-                    first, second = w_real * m_real, w_imag * m_imag
-                    mixed = w_real * m_imag + w_imag * m_real
-                    straight = first if straight is None else straight + first
-                    crossed = second if crossed is None else crossed + second
-                    turned = mixed if turned is None else turned + mixed
-                sbuf[k, 0, row, col] = straight - crossed
-                sbuf[k, 1, row, col] = turned
-            return carry
-
-        lax.fori_loop(0, nmu // rows, one, 0)
-
     def back(channel, k):
         v_real, v_imag = vals[REACH, 0, k], vals[REACH, 1, k]
         summed = dot_nt(sbuf[k, 0], jnp.concatenate([v_real, v_imag], axis=0))
@@ -365,11 +394,10 @@
         backs[channel, k] = jnp.transpose(summed)
 
     gather(0, late)
-    load_s.wait()
-    screen(0)
+    screen(0, late, False)
     back(0, 0)
     second_stage()
-    screen(1)
+    screen(1, late, False)
     back(0, 1)
 
     rs_at = take("recv", 2 * KDEV)
@@ -417,20 +445,21 @@
 
     pairs(1, REACH)
     gather(1, (mate_here,) + late)
+    everything = tuple(range(SLOTS))
+    screen(0, everything, True)
+    back(1, 0)
     u_real, u_imag = last_stage()
+    produce(1, 0, u_real, u_imag)
+    screen(1, everything, True)
+    back(1, 1)
+    produce(1, 1, u_real, u_imag)
+    load_e.wait()
+    complete(1, 0)
     produce(0, 0, u_real, u_imag)
     produce(0, 1, u_real, u_imag)
-    screen(0)
-    back(1, 0)
-    produce(1, 0, u_real, u_imag)
-    screen(1)
-    back(1, 1)
-    load_e.wait()
-    complete(1, 0)
-    produce(1, 1, u_real, u_imag)
+    complete(1, 1)
     complete(0, 0)
     complete(0, 1)
-    complete(1, 1)
 
     @pl.when(pm == 0)
     def _():

time: 67.4 us -> 63.7 us (0.945); the launches traced: 66.3 us -> 63.6 us
  Pallas kernels: 64.8 us -> 62 us
    pallas_call x1, Pallas kernels: 64.8 us -> 62 us  [per_device(): pl.pallas_call(functools.partial(kernel, grid), out_shape=jax.ShapeDtypeS...]
where the time goes in v4:
time: 63.7 us; the launch traced here: 63.6 us
  Pallas kernels  62 us (97%)
  local copies, waits for them, and re-layouts  1.57 us (2%)
    pallas_call x1, Pallas kernels, per_device(): pl.pallas_call(functools.partial(kernel, grid), out_shape=jax.ShapeDtypeS...  62 us
    unnamed x1, local copies, waits for them, and re-layouts  1.57 us

profile of v4, /device:TPU:25, one launch (start us, length us, event | category | flops | bytes accessed | tf_op | source)
XLA Modules:
  0.0 63.6 jit_solution(8022207593490829618)
XLA Ops:
  0.0 62.0 %shard_map.82 = bf16[1,2,2,2,64,128]{5,4,3,2,1,0:T(8,128)(2,1)} custom-call(bf16[1,2,2,2,64,256]{5,4,3,2,1,0:T(8,128)(2,1)} %amps.1, bf16[2,2,256,256]{3,2,1,0:T(8,128)(2,1)} %cond_hbm.1, bf16[2,2,64,512]{3,2,1,0:T(8,128)(2,1)} %val_hbm.1, f32[2,64,128]{2,1,0:T(8,128)} %energy_hbm.1, bf16[4,2,256,512]{3,2,1,0:T(8,128)(2,1)} %screened_hbm.1, ...), custom_call_target="tpu_custom_call" | custom-call | tf_op jit(solution)/shard_map/pallas_call | solution.py:505
  62.0 1.6 %copy.10 = bf16[1,2,2,2,64,128]{5,4,3,2,1,0:T(8,128)(2,1)} copy(bf16[1,2,2,2,64,128]{5,4,3,2,1,0:T(8,128)(2,1)} %shard_map.82) | data formatting | bytes 262144

commit v5 on v4

--- a/solution.py
+++ b/solution.py
@@ -444,13 +444,15 @@
                 copy.start()
 
     pairs(1, REACH)
-    gather(1, (mate_here,) + late)
-    everything = tuple(range(SLOTS))
-    screen(0, everything, True)
+    gather(1, (mate_here,))
+    for k in range(KDEV):
+        screen(k, (REACH, mate_here), True)
+    gather(1, late)
+    screen(0, late, False)
     back(1, 0)
     u_real, u_imag = last_stage()
     produce(1, 0, u_real, u_imag)
-    screen(1, everything, True)
+    screen(1, late, False)
     back(1, 1)
     produce(1, 1, u_real, u_imag)
     load_e.wait()

time: 63.7 us -> 62.8 us (0.986)
  Pallas kernels: 62 us -> 61.1 us
    pallas_call x1, Pallas kernels: 62 us -> 61.1 us  [per_device(): pl.pallas_call(functools.partial(kernel, grid), out_shape=jax.ShapeDtypeS...]
where the time goes in v5:
time: 62.8 us; the launch traced here: 62.7 us
  Pallas kernels  61.1 us (97%)
  local copies, waits for them, and re-layouts  1.57 us (2%)
    pallas_call x1, Pallas kernels, per_device(): pl.pallas_call(functools.partial(kernel, grid), out_shape=jax.ShapeDtypeS...  61.1 us
    unnamed x1, local copies, waits for them, and re-layouts  1.57 us

profile of v5, /device:TPU:25, one launch (start us, length us, event | category | flops | bytes accessed | tf_op | source)
XLA Modules:
  0.0 62.7 jit_solution(5605131129113555265)
XLA Ops:
  0.0 61.1 %shard_map.82 = bf16[1,2,2,2,64,128]{5,4,3,2,1,0:T(8,128)(2,1)} custom-call(bf16[1,2,2,2,64,256]{5,4,3,2,1,0:T(8,128)(2,1)} %amps.1, bf16[2,2,256,256]{3,2,1,0:T(8,128)(2,1)} %cond_hbm.1, bf16[2,2,64,512]{3,2,1,0:T(8,128)(2,1)} %val_hbm.1, f32[2,64,128]{2,1,0:T(8,128)} %energy_hbm.1, bf16[4,2,256,512]{3,2,1,0:T(8,128)(2,1)} %screened_hbm.1, ...), custom_call_target="tpu_custom_call" | custom-call | tf_op jit(solution)/shard_map/pallas_call | solution.py:507
  61.1 1.6 %copy.10 = bf16[1,2,2,2,64,128]{5,4,3,2,1,0:T(8,128)(2,1)} copy(bf16[1,2,2,2,64,128]{5,4,3,2,1,0:T(8,128)(2,1)} %shard_map.82) | data formatting | bytes 262144

commit v6 on v5

--- a/solution.py
+++ b/solution.py
@@ -141,10 +141,8 @@
         device(pm=1 - pm),
         device(pm=0, ka=across),
         device(pm=1, ka=across),
-        device(isdf=1 - side),
         device(ka=above),
         device(ka=below),
-        device(ka=mate),
     ]
     greeted += [device(**a_peer(step)) for step in range(1, a_size)]
     greeted += [device(**b_peer(step)) for step in range(1, nz)]
@@ -186,9 +184,8 @@
 
     @pl.when(pm == 1)
     def _():
-        for part in range(2):
-            send_hop[part].start()
-            send_y[part].start()
+        for copy in send_hop + send_y:
+            copy.start()
 
     @pl.when(pm == 0)
     def _():

time: 62.8 us -> 62.8 us (level)
  no operation moved by 1% of the time
where the time goes in v6:
time: 62.8 us; the launch traced here: 62.6 us
  Pallas kernels  61.1 us (97%)
  local copies, waits for them, and re-layouts  1.57 us (2%)
    pallas_call x1, Pallas kernels, per_device(): pl.pallas_call(functools.partial(kernel, grid), out_shape=jax.ShapeDtypeS...  61.1 us
    unnamed x1, local copies, waits for them, and re-layouts  1.57 us

profile of v6, /device:TPU:25, one launch (start us, length us, event | category | flops | bytes accessed | tf_op | source)
XLA Modules:
  0.0 62.6 jit_solution(18362933255045948770)
XLA Ops:
  0.0 61.1 %shard_map.82 = bf16[1,2,2,2,64,128]{5,4,3,2,1,0:T(8,128)(2,1)} custom-call(bf16[1,2,2,2,64,256]{5,4,3,2,1,0:T(8,128)(2,1)} %amps.1, bf16[2,2,256,256]{3,2,1,0:T(8,128)(2,1)} %cond_hbm.1, bf16[2,2,64,512]{3,2,1,0:T(8,128)(2,1)} %val_hbm.1, f32[2,64,128]{2,1,0:T(8,128)} %energy_hbm.1, bf16[4,2,256,512]{3,2,1,0:T(8,128)(2,1)} %screened_hbm.1, ...), custom_call_target="tpu_custom_call" | custom-call | tf_op jit(solution)/shard_map/pallas_call | solution.py:504
  61.1 1.6 %copy.10 = bf16[1,2,2,2,64,128]{5,4,3,2,1,0:T(8,128)(2,1)} copy(bf16[1,2,2,2,64,128]{5,4,3,2,1,0:T(8,128)(2,1)} %shard_map.82) | data formatting | bytes 262144
